TPU v7x, 32 devices: a whole 2x2x4 slice. The times are simulated.
32 devices in a mesh: clip: 2 (over y), tm: 4 (over z), band: 2 (over x), head: 2 (over core).
Axes of the slice: x: 2, y: 2, z: 4, core: 2. Of those that a mesh axis runs over, the one named last changes fastest.
Arguments:
- queries: bfloat16 [8, 2, 256, 1536], P(('clip', 'tm'), 'band', None, 'head'), parts along dimension 0, may hold values from -6 to 6
- keys: bfloat16 [8, 2, 256, 1536], P(('clip', 'tm'), 'band', None, 'head'), parts along dimension 0, may hold values from -6 to 6
- values: bfloat16 [8, 2, 256, 1536], P(('clip', 'tm'), 'band', None, 'head'), parts along dimension 0, may hold values from -6 to 6
- adj_mask: int32 [8, 2, 2, 2], P(('clip', 'tm'), 'band'), parts along dimension 0, may hold values from 0 to 1, as said below
- border_blocks: int32 [8, 2, 2, 1], P(('clip', 'tm'), 'band'), parts along dimension 0, may hold values from 0 to 1
Outputs:
- attended: bfloat16 [8, 2, 256, 1536], P(('clip', 'tm'), 'band', None, 'head'), parts along dimension 0
There are 2 independent parts, one for each index of `clip`. A program takes and returns all parts, laid end to end along the dimension named above; each array names one. Nothing has to cross between parts.
Inputs may be any that keep to these rules, and one draw needn't show every extreme that they name: `adj_mask`: for each slab, band and direction exactly 1 of the 2 entries are 1.
All inputs are finite; a program needn't handle non-finite values.
Results may differ from a plain program's by a relative error of at most 0.0043.
Values may be sent and summed in bfloat16 or wider, within the bound.
No kernel may reach another device: no remote copies, remote signals or barrier semaphores. Data moves between devices by JAX's collectives and lax.ppermute only.
A program may use at most 64 MiB of HBM per device.

v0:
```python
import math

import jax
import jax.numpy as jnp
from jax import lax
from jax.sharding import PartitionSpec as P

BLK = 128
BSEL = 1
HD = 128


masked_score = -1e30


def with_halo(array, sides, width):
    for axis, dim in sides:
        devices, length = (lax.axis_size(axis), array.shape[dim])
        up = [(i, (i + 1) % devices) for i in range(devices - 1)]
        down = [(j, i) for i, j in up]
        last = lax.slice_in_dim(array, length - width, length, axis=dim)
        first = lax.slice_in_dim(array, 0, width, axis=dim)
        before = lax.ppermute(last, axis, up)
        after = lax.ppermute(first, axis, down)
        array = jnp.concatenate([before, array, after], axis=dim)
    return array


def from_behind(value, axis, steps):
    count = lax.axis_size(axis)
    first, last = (max(0, -steps), min(count, count - steps))
    return lax.ppermute(value, axis, [(source, source + steps) for source in range(first, last)])


def attend(query_heads, key_rows, value_rows, bias, head_count):
    length = key_rows.shape[0]
    key_heads = key_rows.reshape(length, head_count, HD)
    value_heads = value_rows.reshape(length, head_count, HD)
    scores = (
        jnp.einsum("qhd,khd->hqk", query_heads, key_heads, preferred_element_type=jnp.float32)
        * (1.0 / math.sqrt(HD))
        + bias
    )
    maxima = jnp.max(scores, axis=2)
    weights = jnp.exp(scores - maxima[:, :, None])
    totals = jnp.sum(weights, axis=2)
    output = jnp.einsum(
        "hqk,khd->qhd",
        weights.astype(jnp.bfloat16),
        value_heads,
        preferred_element_type=jnp.float32,
    )
    return (maxima, totals, output)


def combine_sources(pieces):
    maxima = jnp.stack([piece[0] for piece in pieces])
    largest = jnp.max(maxima, axis=0)
    factors = jnp.exp(maxima - largest)
    numerator = factors[0].T[:, :, None] * pieces[0][2]
    for number in range(1, len(pieces)):
        numerator = numerator + factors[number].T[:, :, None] * pieces[number][2]
    denominator = jnp.sum(factors * jnp.stack([piece[1] for piece in pieces]), axis=0)
    return numerator / denominator.T[:, :, None]


def block_bias(mask_row, valid):
    return jnp.where(jnp.repeat(mask_row == 1, BLK) & valid, 0.0, masked_score).astype(jnp.float32)


def edge_bias(length, valid):
    return jnp.where(
        valid, jnp.zeros((length,), jnp.float32), jnp.full((length,), masked_score, jnp.float32)
    )


def per_device(queries, keys, values, adj_mask, border_blocks):
    row_count = queries.shape[2]
    feature_width = queries.shape[3]
    head_count = feature_width // HD
    blocks = row_count // BLK
    query_heads = queries[0, 0].reshape(row_count, head_count, HD)
    key_rows = keys[0, 0]
    value_rows = values[0, 0]
    slab_mask = adj_mask[0, 0]
    border_pick = border_blocks[0, 0]
    slab_index = lax.axis_index("tm")
    slab_count = lax.axis_size("tm")
    band_index = lax.axis_index("band")
    band_count = lax.axis_size("band")
    key_blocks = key_rows.reshape(blocks, BLK, feature_width)
    value_blocks = value_rows.reshape(blocks, BLK, feature_width)
    border_order = border_pick.reshape(-1)
    outgoing = jnp.stack(
        [
            jnp.take(key_blocks, border_order, axis=0).reshape(-1, feature_width),
            jnp.take(value_blocks, border_order, axis=0).reshape(-1, feature_width),
        ]
    )
    rim_rows = BSEL * BLK
    widened = with_halo(outgoing, (("band", 1),), rim_rows)
    own_piece = attend(
        query_heads, key_rows, value_rows, jnp.zeros((row_count,), jnp.float32), head_count
    )
    prev_keys, prev_values, prev_mask = from_behind((key_rows, value_rows, slab_mask[0]), "tm", 1)
    next_keys, next_values, next_mask = from_behind((key_rows, value_rows, slab_mask[1]), "tm", -1)
    prev_bias = block_bias(prev_mask, slab_index > 0)
    next_bias = block_bias(next_mask, slab_index < slab_count - 1)
    prev_piece = attend(query_heads, prev_keys, prev_values, prev_bias, head_count)
    next_piece = attend(query_heads, next_keys, next_values, next_bias, head_count)
    lower_piece = attend(
        query_heads,
        widened[0, :rim_rows],
        widened[1, :rim_rows],
        edge_bias(rim_rows, band_index > 0),
        head_count,
    )
    upper_piece = attend(
        query_heads,
        widened[0, -rim_rows:],
        widened[1, -rim_rows:],
        edge_bias(rim_rows, band_index < band_count - 1),
        head_count,
    )
    merged = combine_sources([own_piece, prev_piece, next_piece, lower_piece, upper_piece])
    return merged.reshape(row_count, feature_width).astype(jnp.bfloat16)[None, None]


def solution(mesh):
    placed = (
        P(("clip", "tm"), "band", None, "head"),
        P(("clip", "tm"), "band", None, "head"),
        P(("clip", "tm"), "band", None, "head"),
        P(("clip", "tm"), "band", None, None),
        P(("clip", "tm"), "band", None, None),
    )
    return jax.shard_map(
        per_device,
        mesh=mesh,
        in_specs=placed,
        out_specs=P(("clip", "tm"), "band", None, "head"),
        check_vma=False,
    )
```

profile of v0, /device:TPU:0, one launch (start us, length us, event | category | flops | bytes accessed | tf_op | source)
XLA Modules:
  0.0 61.2 jit_solution(8620650550110630350)
XLA Ops:
  0.0 2.0 %copy.46 = bf16[1,1,256,768]{2,3,1,0:T(8,128)(2,1)} copy(bf16[1,1,256,768]{3,2,1,0:T(8,128)(2,1)} %param.8) | data formatting | bytes 786432 | tf_op args[1]
  2.0 4.9 %collective-permute-start = (bf16[256,768]{0,1:T(8,128)(2,1)}, bf16[256,768]{0,1:T(8,128)(2,1)S(1)}, u32[]{:S(2)}, u32[]{:S(2)}) collective-permute-start(bf16[256,768]{0,1:T(8,128)(2,1)} %bitcast.3), channel_id=1, source_target_pairs={{0,4},{4,8},{8,12},{1,5},{5,9},{9,13},{2,6},{6,10},{10,14},{3,7},{... | collective-permute-start | bytes 1179656 | tf_op jit(solution)/shard_map/ppermute | solution.py:32
  6.9 1.3 %collective-permute-start.2 = (bf16[256,768]{0,1:T(8,128)(2,1)}, bf16[256,768]{0,1:T(8,128)(2,1)}, u32[]{:S(2)}, u32[]{:S(2)}) collective-permute-start(bf16[256,768]{0,1:T(8,128)(2,1)} %bitcast.3), channel_id=1, source_target_pairs={{4,0},{8,4},{12,8},{5,1},{9,5},{13,9},{6,2},{10,6},{14,10},{7,3},{... | collective-permute-start | bytes 1179656 | tf_op jit(solution)/shard_map/ppermute | solution.py:32
  8.2 1.3 %collective-permute-start.7 = (bf16[256,768]{1,0:T(8,128)(2,1)}, bf16[256,768]{1,0:T(8,128)(2,1)}, u32[]{:S(2)}, u32[]{:S(2)}) collective-permute-start(bf16[256,768]{1,0:T(8,128)(2,1)} %bitcast.128), channel_id=1, source_target_pairs={{4,0},{8,4},{12,8},{5,1},{9,5},{13,9},{6,2},{10,6},{14,10},{7,3},{... | collective-permute-start | bytes 1179656 | tf_op jit(solution)/shard_map/ppermute | solution.py:32
  9.5 5.9 %collective-permute-start.6 = (bf16[256,768]{1,0:T(8,128)(2,1)}, bf16[256,768]{1,0:T(8,128)(2,1)}, u32[]{:S(2)}, u32[]{:S(2)}) collective-permute-start(bf16[256,768]{1,0:T(8,128)(2,1)} %bitcast.129), channel_id=1, source_target_pairs={{0,4},{4,8},{8,12},{1,5},{5,9},{9,13},{2,6},{6,10},{10,14},{3,7},{... | collective-permute-start | bytes 1179656 | tf_op jit(solution)/shard_map/ppermute | solution.py:32
  15.5 0.8 %slice_bitcast_fusion.5 = (s32[2]{0:T(128)S(1)}, s32[2]{0:T(128)S(1)}) fusion(s32[1,1,2,2]{3,2,1,0:T(2,128)} %param.10), kind=kLoop, calls=%fused_computation.76 | loop fusion | bytes 32 | tf_op jit(solution)/shard_map/squeeze | solution.py:106
  16.2 3.8 %collective-permute-start.1 = (s32[2]{0:T(128)S(1)}, s32[2]{0:T(128)}, u32[]{:S(2)}, u32[]{:S(2)}) collective-permute-start(s32[2]{0:T(128)S(1)} %get-tuple-element.20), channel_id=1, source_target_pairs={{0,4},{4,8},{8,12},{1,5},{5,9},{9,13},{2,6},{6,10},{10,14},{3,7},{... | collective-permute-start | bytes 32 | tf_op jit(solution)/shard_map/ppermute | solution.py:32
  20.0 0.7 %compare_select_fusion = s32[2]{0:T(128)S(1)} fusion(s32[1,1,2,1]{2,3,1,0:T(1,128)} %param.11), kind=kLoop, calls=%fused_computation.72 | loop fusion | flops 6 | bytes 16 | tf_op jit(solution)/shard_map/jit(_take)/jit(_where)/select_n | solution.py:96
  20.6 0.7 %compare_and_fusion = pred[2]{0:T(512)(128)(4,1)S(1)} fusion(s32[1,1,2,1]{2,3,1,0:T(1,128)} %param.11), kind=kLoop, calls=%fused_computation.73 | loop fusion | flops 12 | bytes 10 | tf_op jit(solution)/shard_map/jit(_take)/and | solution.py:96
  21.3 1.9 %copy.60 = bf16[1,1,256,768]{2,3,1,0:T(8,128)(2,1)} copy(bf16[1,1,256,768]{3,2,1,0:T(8,128)(2,1)} %param.9) | data formatting | bytes 786432 | tf_op args[2]
  23.3 0.6 gather_fusion
  23.8 0.6 gather_fusion.1
  24.4 0.1 broadcast_select_fusion.1
  24.6 0.2 copy.54
  24.8 0.2 copy.55
  24.9 0.5 copy-done.7
  25.4 0.2 copy.45
  25.6 1.4 %fusion.39 = (f32[6,256]{1,0:T(8,128)S(1)}, f32[6,256,256]{1,2,0:T(8,128)S(1)}) fusion(bf16[256,6,128]{0,2,1:T(8,128)(2,1)S(1)} %bitcast.122, bf16[256,6,128]{0,2,1:T(8,128)(2,1)} %bitcast.1), kind=kOutput, calls=%fused_computation.83 | convolution fusion | flops 101448192 | bytes 2365440 | tf_op jit(solution)/shard_map/qhd,khd->hqk/dot_general | solution.py:40
  27.0 0.6 constant_dynamic-update-slice_fusion.4
  27.6 0.2 fusion
  27.9 0.1 fusion.33
  28.0 1.3 %collective-permute-start.3 = (s32[2]{0:T(128)S(1)}, s32[2]{0:T(128)S(1)}, u32[]{:S(2)}, u32[]{:S(2)}) collective-permute-start(s32[2]{0:T(128)S(1)} %get-tuple-element.19), channel_id=1, source_target_pairs={{4,0},{8,4},{12,8},{5,1},{9,5},{13,9},{6,2},{10,6},{14,10},{7,3},{... | collective-permute-start | bytes 32 | tf_op jit(solution)/shard_map/ppermute | solution.py:32
  29.3 0.7 %and_select_fusion.1 = f32[2]{0:T(128)S(1)} fusion(s32[2]{0:T(128)} %collective-permute-done.1, pred[]{:T(512)S(6)} %gt.6), kind=kLoop, calls=%fused_computation.75 | loop fusion | flops 6 | bytes 17 | tf_op jit(solution)/shard_map/jit(_where)/select_n | solution.py:68
  30.0 0.1 broadcast_bitcast_fusion.1
  30.1 3.4 %collective-permute-done.3 = s32[2]{0:T(128)S(1)} collective-permute-done((s32[2]{0:T(128)S(1)}, s32[2]{0:T(128)S(1)}, u32[]{:S(2)}, u32[]{:S(2)}) %collective-permute-start.3) | collective-permute-done | bytes 40 | tf_op jit(solution)/shard_map/ppermute | solution.py:32
  33.5 1.3 %collective-permute-start.5 = (bf16[2,128,768]{1,2,0:T(8,128)(2,1)S(1)}, bf16[2,128,768]{1,2,0:T(8,128)(2,1)S(1)}, u32[]{:S(2)}, u32[]{:S(2)}) collective-permute-start(bf16[2,128,768]{1,2,0:T(8,128)(2,1)S(1)} %get-tuple-element.9), channel_id=1, source_target_pairs={{2,0},{3,1},{6,4},{7,5},{10,8},{11,9},{14,12},{15,13},{18,16},{19,... | collective-permute-start | bytes 1179656 | tf_op jit(solution)/shard_map/ppermute | solution.py:24
  34.8 4.6 %collective-permute-start.4 = (bf16[2,128,768]{1,2,0:T(8,128)(2,1)S(1)}, bf16[2,128,768]{1,2,0:T(8,128)(2,1)S(1)}, u32[]{:S(2)}, u32[]{:S(2)}) collective-permute-start(bf16[2,128,768]{1,2,0:T(8,128)(2,1)S(1)} %get-tuple-element.8), channel_id=1, source_target_pairs={{0,2},{1,3},{4,6},{5,7},{8,10},{9,11},{12,14},{13,15},{16,18},{17,... | collective-permute-start | bytes 1179656 | tf_op jit(solution)/shard_map/ppermute | solution.py:23
  39.4 1.4 %fusion.40 = (f32[6,256]{1,0:T(8,128)S(1)}, f32[6,256,256]{1,2,0:T(8,128)S(1)}) fusion(f32[256]{0:T(256)S(1)} %broadcast_bitcast_fusion.1, bf16[256,6,128]{0,2,1:T(8,128)(2,1)S(1)} %bitcast.123, bf16[256,6,128]{0,2,1:T(8,128)(2,1)} %bitcast.141), kind=kOutput, calls=%fused_computation.84 | convolution fusion | flops 101841408 | bytes 2366464 | tf_op jit(solution)/shard_map/qhd,khd->hqk/dot_general | solution.py:40
  40.9 1.4 %fusion.41 = (f32[6,256]{1,0:T(8,128)S(1)}, f32[6,256,256]{1,2,0:T(8,128)S(1)}) fusion(f32[256]{0:T(256)S(1)} %broadcast_bitcast_fusion, bf16[256,6,128]{0,2,1:T(8,128)(2,1)S(1)} %bitcast.124, bf16[256,6,128]{0,2,1:T(8,128)(2,1)} %bitcast.8), kind=kOutput, calls=%fused_computation.85 | convolution fusion | flops 101841408 | bytes 2366464 | tf_op jit(solution)/shard_map/qhd,khd->hqk/dot_general | solution.py:40
  42.3 0.2 fusion.2
  42.6 2.3 %collective-permute-done.4 = bf16[2,128,768]{1,2,0:T(8,128)(2,1)S(1)} collective-permute-done((bf16[2,128,768]{1,2,0:T(8,128)(2,1)S(1)}, bf16[2,128,768]{1,2,0:T(8,128)(2,1)S(1)}, u32[]{:S(2)}, u32[]{:S(2)}) %collective-permute-start.4) | collective-permute-done | bytes 393248 | tf_op jit(solution)/shard_map/ppermute | solution.py:23
  44.9 0.7 %fusion.36 = (bf16[1,128,768]{1,2,0:T(8,128)(2,1)}, bf16[1,128,768]{1,2,0:T(8,128)(2,1)S(1)}) fusion(bf16[2,128,768]{1,2,0:T(8,128)(2,1)S(1)} %collective-permute-done.4), kind=kLoop, calls=%fused_computation.80 | loop fusion | bytes 786432 | tf_op jit(solution)/shard_map/slice | solution.py:114
  45.6 0.3 fusion.42
  46.0 0.8 %copy-done.1 = f32[6,256,128]{1,2,0:T(8,128)} copy-done((f32[6,256,128]{1,2,0:T(8,128)}, f32[6,256,128]{1,2,0:T(8,128)S(1)}, u32[]{:S(2)}) %copy-start.1) | copy-done | bytes 786456
  46.8 0.1 fusion.27
  47.0 0.2 fusion.4
  47.2 0.3 fusion.38
  47.6 0.1 fusion.29
  47.8 0.6 multiply_reduce_fusion
  48.4 0.6 %slice_bitcast_fusion.3 = (f32[256,6]{0,1:T(8,128)}, f32[256,6]{0,1:T(8,128)S(1)}, f32[256,6]{0,1:T(8,128)}, f32[256,6]{0,1:T(8,128)}, f32[256,6]{0,1:T(8,128)}) fusion(f32[5,6,256]{2,1,0:T(8,128)S(1)} %get-tuple-element.7), kind=kLoop, calls=%fused_computation.68 | loop fusion | bytes 61440 | tf_op jit(solution)/shard_map/transpose | solution.py:62
  49.0 1.2 %fusion.14 = f32[256,6,128]{0,2,1:T(8,128)} fusion(bf16[128,6,128]{0,2,1:T(8,128)(2,1)S(1)} %bitcast.138, f32[6,256,128]{1,2,0:T(8,128)S(1)} %get-tuple-element.24, f32[6,256]{1,0:T(8,128)S(1)} %get-tuple-element.23, f32[256,6]{0,1:T(8,128)S(1)} %get-tuple-element.15), kind=kOutput, calls=%fused_computation.26 | convolution fusion | flops 50921472 | bytes 1781760 | tf_op jit(solution)/shard_map/hqk,khd->qhd/dot_general | solution.py:47
  50.2 1.2 %copy.64 = bf16[256,768]{0,1:T(8,128)(2,1)S(1)} copy(bf16[256,768]{1,0:T(8,128)(2,1)} %collective-permute-done.7) | data formatting | bytes 786432 | tf_op jit(solution)/shard_map/ppermute | solution.py:32
  51.4 2.8 %fusion.13 = f32[256,6,128]{0,2,1:T(8,128)} fusion(bf16[256,6,128]{0,2,1:T(8,128)(2,1)S(1)} %bitcast.134, f32[6,256,256]{1,2,0:T(8,128)} %copy-done, f32[6,256]{1,0:T(8,128)} %copy-done.9, f32[256,6]{0,1:T(8,128)} %get-tuple-element.17), kind=kOutput, calls=%fused_computation.24 | convolution fusion | flops 101646336 | bytes 2764800 | tf_op jit(solution)/shard_map/hqk,khd->qhd/dot_general | solution.py:47
  54.3 1.2 %fusion.15 = f32[256,6,128]{0,2,1:T(8,128)} fusion(bf16[128,6,128]{0,2,1:T(8,128)(2,1)S(1)} %bitcast.137, f32[6,256,128]{1,2,0:T(8,128)S(1)} %copy-done.2, f32[6,256]{1,0:T(8,128)S(1)} %copy-done.11, f32[256,6]{0,1:T(8,128)S(1)} %copy-done.16), kind=kOutput, calls=%fused_computation.28 | convolution fusion | flops 50921472 | bytes 1781760 | tf_op jit(solution)/shard_map/hqk,khd->qhd/dot_general | solution.py:47
  55.5 1.3 %fusion.6 = f32[256,6,128]{0,2,1:T(8,128)} fusion(bf16[256,6,128]{0,2,1:T(8,128)(2,1)S(1)} %bitcast.133, f32[6,256,256]{1,2,0:T(8,128)S(1)} %get-tuple-element.26, f32[6,256]{1,0:T(8,128)S(1)} %get-tuple-element.25, f32[256,6]{0,1:T(8,128)S(1)} %copy-done.15), kind=kOutput, calls=%fused_computation.17 | convolution fusion | flops 101646336 | bytes 2764800 | tf_op jit(solution)/shard_map/hqk,khd->qhd/dot_general | solution.py:47
  56.8 1.2 %copy.62 = bf16[256,768]{0,1:T(8,128)(2,1)S(1)} copy(bf16[256,768]{1,0:T(8,128)(2,1)} %collective-permute-done.6) | data formatting | bytes 786432 | tf_op jit(solution)/shard_map/ppermute | solution.py:32
  58.0 2.3 %fusion.20 = bf16[256,6,128]{0,2,1:T(8,128)(2,1)S(1)} fusion(f32[256,6,128]{0,2,1:T(8,128)} %fusion.14, f32[256,6,128]{0,2,1:T(8,128)} %fusion.15, f32[256,6,128]{0,2,1:T(8,128)} %fusion.13, f32[256,6,128]{0,2,1:T(8,128)} %fusion.6, bf16[256,6,128]{0,2,1:T(8,128)(2,1)S(1)} %bitcast.135, f32[6,256,256]{1,2,0:T(8,128)S(1)} %get-tuple-element.28, ...), kind=kOutput, calls=%fused_computation.35 | convolution fusion | flops 102825984 | bytes 5523456 | tf_op jit(solution)/shard_map/hqk,khd->qhd/dot_general | solution.py:47
  60.2 0.9 %copy.68 = bf16[1,1,256,768]{3,2,1,0:T(8,128)(2,1)} copy(bf16[1,1,256,768]{2,3,1,0:T(8,128)(2,1)S(1)} %bitcast.136) | data formatting | bytes 786432 | tf_op jit(solution)/shard_map/convert_element_type | solution.py:126
  (51 shorter events, 0.2 us)
Async XLA Ops:
  0.0 23.3 %copy-start.3 = (bf16[1,1,256,768]{3,2,1,0:T(8,128)(2,1)S(1)}, bf16[1,1,256,768]{3,2,1,0:T(8,128)(2,1)}, u32[]{:S(2)}) copy-start(bf16[1,1,256,768]{3,2,1,0:T(8,128)(2,1)} %param.8) | copy-start | bytes 1179652
  0.0 23.8 %copy-start.4 = (bf16[1,1,256,768]{3,2,1,0:T(8,128)(2,1)S(1)}, bf16[1,1,256,768]{3,2,1,0:T(8,128)(2,1)}, u32[]{:S(2)}) copy-start(bf16[1,1,256,768]{3,2,1,0:T(8,128)(2,1)} %param.9) | copy-start | bytes 1179652
  2.0 32.8 %collective-permute-start = (bf16[256,768]{0,1:T(8,128)(2,1)}, bf16[256,768]{0,1:T(8,128)(2,1)S(1)}, u32[]{:S(2)}, u32[]{:S(2)}) collective-permute-start(bf16[256,768]{0,1:T(8,128)(2,1)} %bitcast.3), channel_id=1, source_target_pairs={{0,4},{4,8},{8,12},{1,5},{5,9},{9,13},{2,6},{6,10},{10,14},{3,7},{... | collective-permute-start | bytes 1179656 | tf_op jit(solution)/shard_map/ppermute | solution.py:32
  6.9 34.0 %collective-permute-start.2 = (bf16[256,768]{0,1:T(8,128)(2,1)}, bf16[256,768]{0,1:T(8,128)(2,1)}, u32[]{:S(2)}, u32[]{:S(2)}) collective-permute-start(bf16[256,768]{0,1:T(8,128)(2,1)} %bitcast.3), channel_id=1, source_target_pairs={{4,0},{8,4},{12,8},{5,1},{9,5},{13,9},{6,2},{10,6},{14,10},{7,3},{... | collective-permute-start | bytes 1179656 | tf_op jit(solution)/shard_map/ppermute | solution.py:32
  8.2 42.0 %collective-permute-start.7 = (bf16[256,768]{1,0:T(8,128)(2,1)}, bf16[256,768]{1,0:T(8,128)(2,1)}, u32[]{:S(2)}, u32[]{:S(2)}) collective-permute-start(bf16[256,768]{1,0:T(8,128)(2,1)} %bitcast.128), channel_id=1, source_target_pairs={{4,0},{8,4},{12,8},{5,1},{9,5},{13,9},{6,2},{10,6},{14,10},{7,3},{... | collective-permute-start | bytes 1179656 | tf_op jit(solution)/shard_map/ppermute | solution.py:32
  9.5 47.2 %collective-permute-start.6 = (bf16[256,768]{1,0:T(8,128)(2,1)}, bf16[256,768]{1,0:T(8,128)(2,1)}, u32[]{:S(2)}, u32[]{:S(2)}) collective-permute-start(bf16[256,768]{1,0:T(8,128)(2,1)} %bitcast.129), channel_id=1, source_target_pairs={{0,4},{4,8},{8,12},{1,5},{5,9},{9,13},{2,6},{6,10},{10,14},{3,7},{... | collective-permute-start | bytes 1179656 | tf_op jit(solution)/shard_map/ppermute | solution.py:32
  16.2 11.8 %collective-permute-start.1 = (s32[2]{0:T(128)S(1)}, s32[2]{0:T(128)}, u32[]{:S(2)}, u32[]{:S(2)}) collective-permute-start(s32[2]{0:T(128)S(1)} %get-tuple-element.20), channel_id=1, source_target_pairs={{0,4},{4,8},{8,12},{1,5},{5,9},{9,13},{2,6},{6,10},{10,14},{3,7},{... | collective-permute-start | bytes 32 | tf_op jit(solution)/shard_map/ppermute | solution.py:32
  24.4 1.0 %copy-start.7 = (bf16[1,1,256,768]{3,2,1,0:T(8,128)(2,1)S(1)}, bf16[1,1,256,768]{3,2,1,0:T(8,128)(2,1)}, u32[]{:S(2)}) copy-start(bf16[1,1,256,768]{3,2,1,0:T(8,128)(2,1)} %param.7) | copy-start | bytes 1179652
  28.0 12.9 %copy-start.12 = (f32[5,6,256]{2,1,0:T(8,128)S(1)}, f32[5,6,256]{2,1,0:T(8,128)}, u32[]{:S(2)}) copy-start(f32[5,6,256]{2,1,0:T(8,128)} %constant_dynamic-update-slice_fusion.4) | copy-start | bytes 92164
  28.0 5.4 %collective-permute-start.3 = (s32[2]{0:T(128)S(1)}, s32[2]{0:T(128)S(1)}, u32[]{:S(2)}, u32[]{:S(2)}) collective-permute-start(s32[2]{0:T(128)S(1)} %get-tuple-element.19), channel_id=1, source_target_pairs={{4,0},{8,4},{12,8},{5,1},{9,5},{13,9},{6,2},{10,6},{14,10},{7,3},{... | collective-permute-start | bytes 32 | tf_op jit(solution)/shard_map/ppermute | solution.py:32
  33.5 13.7 %collective-permute-start.5 = (bf16[2,128,768]{1,2,0:T(8,128)(2,1)S(1)}, bf16[2,128,768]{1,2,0:T(8,128)(2,1)S(1)}, u32[]{:S(2)}, u32[]{:S(2)}) collective-permute-start(bf16[2,128,768]{1,2,0:T(8,128)(2,1)S(1)} %get-tuple-element.9), channel_id=1, source_target_pairs={{2,0},{3,1},{6,4},{7,5},{10,8},{11,9},{14,12},{15,13},{18,16},{19,... | collective-permute-start | bytes 1179656 | tf_op jit(solution)/shard_map/ppermute | solution.py:24
  34.8 4.6 %copy-start.8 = (bf16[256,768]{0,1:T(8,128)(2,1)}, bf16[256,768]{0,1:T(8,128)(2,1)S(1)}, u32[]{:S(2)}) copy-start(bf16[256,768]{0,1:T(8,128)(2,1)S(1)} %collective-permute-done) | copy-start | bytes 1179652
  34.8 10.1 %collective-permute-start.4 = (bf16[2,128,768]{1,2,0:T(8,128)(2,1)S(1)}, bf16[2,128,768]{1,2,0:T(8,128)(2,1)S(1)}, u32[]{:S(2)}, u32[]{:S(2)}) collective-permute-start(bf16[2,128,768]{1,2,0:T(8,128)(2,1)S(1)} %get-tuple-element.8), channel_id=1, source_target_pairs={{0,2},{1,3},{4,6},{5,7},{8,10},{9,11},{12,14},{13,15},{16,18},{17,... | collective-permute-start | bytes 1179656 | tf_op jit(solution)/shard_map/ppermute | solution.py:23
  42.3 4.6 %copy-start = (f32[6,256,256]{1,2,0:T(8,128)}, f32[6,256,256]{1,2,0:T(8,128)S(1)}, u32[]{:S(2)}) copy-start(f32[6,256,256]{1,2,0:T(8,128)S(1)} %get-tuple-element.30) | copy-start | bytes 4718596
  42.3 5.3 %copy-start.9 = (f32[6,256]{1,0:T(8,128)}, f32[6,256]{1,0:T(8,128)S(1)}, u32[]{:S(2)}) copy-start(f32[6,256]{1,0:T(8,128)S(1)} %get-tuple-element.29) | copy-start | bytes 18436
  46.0 0.9 %copy-start.1 = (f32[6,256,128]{1,2,0:T(8,128)}, f32[6,256,128]{1,2,0:T(8,128)S(1)}, u32[]{:S(2)}) copy-start(f32[6,256,128]{1,2,0:T(8,128)S(1)} %get-tuple-element.32) | copy-start | bytes 2359300
  46.0 1.6 %copy-start.10 = (f32[6,256]{1,0:T(8,128)}, f32[6,256]{1,0:T(8,128)S(1)}, u32[]{:S(2)}) copy-start(f32[6,256]{1,0:T(8,128)S(1)} %get-tuple-element.31) | copy-start | bytes 18436
  51.4 2.8 %copy-start.2 = (f32[6,256,128]{1,2,0:T(8,128)S(1)}, f32[6,256,128]{1,2,0:T(8,128)}, u32[]{:S(2)}) copy-start(f32[6,256,128]{1,2,0:T(8,128)} %copy-done.1) | copy-start | bytes 2359300
  51.4 2.8 %copy-start.6 = (bf16[1,128,768]{1,2,0:T(8,128)(2,1)S(1)}, bf16[1,128,768]{1,2,0:T(8,128)(2,1)}, u32[]{:S(2)}) copy-start(bf16[1,128,768]{1,2,0:T(8,128)(2,1)} %get-tuple-element.10) | copy-start | bytes 589828
  51.4 2.8 %copy-start.11 = (f32[6,256]{1,0:T(8,128)S(1)}, f32[6,256]{1,0:T(8,128)}, u32[]{:S(2)}) copy-start(f32[6,256]{1,0:T(8,128)} %copy-done.10) | copy-start | bytes 18436
  51.4 2.8 %copy-start.16 = (f32[256,6]{0,1:T(8,128)S(1)}, f32[256,6]{0,1:T(8,128)}, u32[]{:S(2)}) copy-start(f32[256,6]{0,1:T(8,128)} %get-tuple-element.16) | copy-start | bytes 18436
  54.2 1.2 %copy-start.5 = (bf16[1,1,256,768]{2,3,1,0:T(8,128)(2,1)S(1)}, bf16[1,1,256,768]{2,3,1,0:T(8,128)(2,1)}, u32[]{:S(2)}) copy-start(bf16[1,1,256,768]{2,3,1,0:T(8,128)(2,1)} %copy.60) | copy-start | bytes 1179652
  54.2 1.2 %copy-start.15 = (f32[256,6]{0,1:T(8,128)S(1)}, f32[256,6]{0,1:T(8,128)}, u32[]{:S(2)}) copy-start(f32[256,6]{0,1:T(8,128)} %get-tuple-element.18) | copy-start | bytes 18436
  55.4 2.5 %copy-start.13 = (f32[6,256]{1,0:T(8,128)S(1)}, f32[6,256]{1,0:T(8,128)}, u32[]{:S(2)}) copy-start(f32[6,256]{1,0:T(8,128)} %get-tuple-element.6) | copy-start | bytes 18436
  55.4 2.5 %copy-start.14 = (f32[256,6]{0,1:T(8,128)S(1)}, f32[256,6]{0,1:T(8,128)}, u32[]{:S(2)}) copy-start(f32[256,6]{0,1:T(8,128)} %get-tuple-element.14) | copy-start | bytes 18436
where the time goes:
time: 61.9 us; the launch traced here: 61.2 us
  starting transfers between devices  24.4 us (39%)
  matrix products  13.7 us (22%)
  local copies, waits for them, and re-layouts  13.1 us (21%)
  waiting for transfers between devices  5.72 us (9%)
  other arithmetic  3.83 us (6%)
    ppermute x6, starting transfers between devices, from_behind(): lax.ppermute(value, axis, [(source, source + steps) for source in range(f...  18.5 us
    dot_general x5, matrix products, attend(): jnp.einsum('hqk,khd->qhd', weights.astype(jnp.bfloat16), value_heads, pre...  8.76 us
    unnamed x45, local copies, waits for them, and re-layouts  6.11 us
    dot_general x5, matrix products, attend(): jnp.einsum('qhd,khd->hqk', query_heads, key_heads, preferred_element_type...  4.92 us
    ppermute x1, starting transfers between devices, with_halo(): before = lax.ppermute(last, axis, up)  4.58 us
    ppermute x6, waiting for transfers between devices, from_behind(): lax.ppermute(value, axis, [(source, source + steps) for source in range(f...  3.39 us
    ppermute x1, waiting for transfers between devices, with_halo(): before = lax.ppermute(last, axis, up)  2.34 us
    ppermute x2, local copies, waits for them, and re-layouts, from_behind(): lax.ppermute(value, axis, [(source, source + steps) for source in range(f...  2.33 us
  transfers between devices with their start and end apart: 8, of which 2 were waited for; matrix products, arithmetic and copies ran while one was open for 37% of the time, Pallas kernels for 0%

commit v1 on v0

v1 whole, which is shorter than its diff:
```python
import functools
import math

import jax
import jax.numpy as jnp
from jax import lax
from jax.experimental import pallas as pl
from jax.experimental.pallas import tpu as pltpu
from jax.sharding import PartitionSpec as P

BLK = 128
HD = 128
MASKED = -1e30
TO_EXP2 = math.log2(math.e) / math.sqrt(HD)


def swaps(axis_sizes):
    return [(axis, phase) for axis, size in axis_sizes for phase in range(min(2, size - 1))]


def swap(value, axis, phase):
    size, spare = lax.axis_size(axis), lax.axis_size("head")
    partner = {}
    for low in range(phase, size - 1, 2):
        partner[low], partner[low + 1] = low + 1, low
    pairs = []
    for here in range(size):
        for head in range(spare):
            if here in partner:
                pairs.append((here * spare + head, partner[here] * spare + head))
            elif spare % 2 == 0:
                pairs.append((here * spare + head, here * spare + (head ^ 1)))
    return lax.ppermute(value, (axis, "head"), pairs)


def pick(plan, adj_mask, border_blocks, keys, values):
    width = keys.shape[1]
    blocks = adj_mask.shape[1]
    counts = [border_blocks.shape[1] if axis == "band" else 1 for axis, _ in plan]

    def kernel(adj_ref, border_ref, key_ref, value_ref, *rest):
        outs, sems = rest[: len(plan)], rest[len(plan)]
        copies = []
        for number, (axis, phase) in enumerate(plan):
            up = lax.rem(lax.axis_index(axis), 2) == phase
            for entry in range(counts[number]):
                if axis == "band":
                    block = border_ref[jnp.where(up, 1, 0), entry]
                else:
                    row = jnp.where(up, 0, 1)
                    block = 0
                    for j in range(1, blocks):
                        block = block + j * adj_ref[row, j]
                rows = pl.ds(pl.multiple_of(block * BLK, BLK), BLK)
                for part, source in enumerate((key_ref, value_ref)):
                    copy = pltpu.make_async_copy(
                        source.at[rows],
                        outs[number].at[pl.ds((part * counts[number] + entry) * BLK, BLK)],
                        sems.at[len(copies)],
                    )
                    copy.start()
                    copies.append(copy)
        for copy in copies:
            copy.wait()

    anywhere = pl.BlockSpec(memory_space=pl.ANY)
    scalar = pl.BlockSpec(memory_space=pltpu.SMEM)
    return pl.pallas_call(
        kernel,
        name="pick",
        out_shape=[pltpu.VMEM((2 * count * BLK, width), keys.dtype) for count in counts],
        in_specs=[scalar, scalar, anywhere, anywhere],
        out_specs=[pl.BlockSpec(memory_space=pltpu.VMEM)] * len(plan),
        scratch_shapes=[pltpu.SemaphoreType.DMA((2 * sum(counts),))],
    )(adj_mask, border_blocks, keys, values)


def score(query, key):
    return lax.dot_general(query, key, (((1,), (1,)), ((), ())), preferred_element_type=jnp.float32) * TO_EXP2


def weigh(weights, value):
    both = jnp.concatenate([value, jnp.ones_like(value)], axis=1)
    return jnp.dot(weights.astype(value.dtype), both, preferred_element_type=jnp.float32)


def own(queries, keys, values):
    rows, width = queries.shape
    heads = width // HD

    def kernel(query_ref, key_ref, value_ref, top_ref, total_ref):
        for head in range(heads):
            cols = slice(head * HD, (head + 1) * HD)
            scores = score(query_ref[:, cols], key_ref[:, cols])
            top = jnp.max(scores, axis=1, keepdims=True)
            total_ref[head] = weigh(jnp.exp2(scores - top), value_ref[:, cols])
            top_ref[head] = jnp.broadcast_to(top, (rows, HD))

    in_vmem = pl.BlockSpec(memory_space=pltpu.VMEM)
    return pl.pallas_call(
        kernel,
        name="own",
        out_shape=[pltpu.VMEM((heads, rows, HD), jnp.float32), pltpu.VMEM((heads, rows, 2 * HD), jnp.float32)],
        in_specs=[in_vmem] * 3,
        out_specs=[in_vmem] * 2,
        cost_estimate=pl.CostEstimate(flops=4 * rows * rows * width, bytes_accessed=6 * rows * width, transcendentals=rows * rows * heads),
    )(queries, keys, values)


def join(queries, swapped, state, axis, phase, last):
    rows, width = queries.shape
    heads = width // HD
    length = swapped.shape[0] // 2
    size = lax.axis_size(axis)

    def kernel(query_ref, swapped_ref, top_ref, total_ref, *outs):
        here = lax.axis_index(axis)
        up = lax.rem(here, 2) == phase
        valid = jnp.where(up, here < size - 1, here > 0)
        bias = jnp.where(valid, 0.0, MASKED).astype(jnp.float32)
        for head in range(heads):
            cols = slice(head * HD, (head + 1) * HD)
            scores = score(query_ref[:, cols], swapped_ref[:length, cols]) + bias
            old_top = top_ref[head]
            top = jnp.maximum(old_top, jnp.max(scores, axis=1, keepdims=True))
            kept = jnp.exp2(old_top - top)
            new = weigh(jnp.exp2(scores - top[:, :1]), swapped_ref[length:, cols])
            total = total_ref[head]
            left = total[:, :HD] * kept + new[:, :HD]
            right = total[:, HD:] * kept + new[:, HD:]
            if last:
                outs[0][:, cols] = (left / right).astype(outs[0].dtype)
            else:
                outs[0][head] = top
                outs[1][head, :, :HD] = left
                outs[1][head, :, HD:] = right

    in_vmem = pl.BlockSpec(memory_space=pltpu.VMEM)
    if last:
        out_shape, out_specs = jax.ShapeDtypeStruct((rows, width), queries.dtype), in_vmem
    else:
        out_shape = [pltpu.VMEM((heads, rows, HD), jnp.float32), pltpu.VMEM((heads, rows, 2 * HD), jnp.float32)]
        out_specs = [in_vmem] * 2
    return pl.pallas_call(
        kernel,
        name="join_" + axis,
        out_shape=out_shape,
        in_specs=[in_vmem] * 4,
        out_specs=out_specs,
        cost_estimate=pl.CostEstimate(flops=4 * rows * length * width, bytes_accessed=6 * rows * width, transcendentals=rows * length * heads),
    )(queries, swapped, *state)


def per_device(queries, keys, values, adj_mask, border_blocks):
    queries, keys, values = queries[0, 0], keys[0, 0], values[0, 0]
    tm, band = lax.axis_size("tm"), lax.axis_size("band")
    plan = swaps((("tm", tm), ("band", band)))
    plan.sort(key=lambda entry: entry[1])
    outgoing = pick(plan, adj_mask[0, 0], border_blocks[0, 0], keys, values)
    incoming = [swap(rows, axis, phase) for rows, (axis, phase) in zip(outgoing, plan)]
    state = own(queries, keys, values)
    for number, (axis, phase) in enumerate(plan):
        state = join(queries, incoming[number], state, axis, phase, number == len(plan) - 1)
    return state[None, None]


def solution(mesh):
    wide = P(("clip", "tm"), "band", None, "head")
    narrow = P(("clip", "tm"), "band", None, None)
    return jax.shard_map(
        per_device, mesh=mesh, in_specs=(wide, wide, wide, narrow, narrow), out_specs=wide, check_vma=False
    )
```

time: 61.9 us -> 30.7 us (0.50)
  starting transfers between devices: 24.4 us -> 4.62 us
  Pallas kernels: 0 us -> 14.7 us
  matrix products: 13.7 us -> 0 us
  local copies, waits for them, and re-layouts: 13.1 us -> 7.42 us
  other arithmetic: 3.83 us -> 0 us
  waiting for transfers between devices: 5.72 us -> 3.65 us
    ppermute x8 -> x3, starting transfers between devices: 24.4 us -> 4.62 us  [swap(): return lax.ppermute(value, (axis, 'head'), pairs)]
    pallas_call x0 -> x5, Pallas kernels: none -> 14.7 us  [the longest x3 10.6 us: join(): pl.pallas_call(kernel, name='join_' + axis, out_shape=out_shape, in_specs...]
    dot_general x10 -> x0, matrix products: 13.7 us -> none  [the longest x5 8.76 us: attend(): jnp.einsum('hqk,khd->qhd', weights.astype(jnp.bfloat16), value_heads, pre...]
    ppermute x2 -> x0, local copies, waits for them, and re-layouts: 2.33 us -> none  [from_behind(): lax.ppermute(value, axis, [(source, source + steps) for source in range(f...]
    ppermute x8 -> x3, waiting for transfers between devices: 5.72 us -> 3.65 us  [swap(): return lax.ppermute(value, (axis, 'head'), pairs)]
    reduce_sum x6 -> x0, other arithmetic: 1.52 us -> none  [the longest x5 0.91 us: attend(): totals = jnp.sum(weights, axis=2)]
    select_n x4 -> x0, other arithmetic: 1.49 us -> none  [the longest x2 0.8 us: per_device(): jnp.take(key_blocks, border_order, axis=0).reshape(-1, feature_width)]
    gather x2 -> x0, local copies, waits for them, and re-layouts: 1.15 us -> none  [the longest x1 0.57 us: per_device(): jnp.take(key_blocks, border_order, axis=0).reshape(-1, feature_width)]
  transfers between devices with their start and end apart: 8 -> 3, of which waited for: 2 -> 1; matrix products, arithmetic and copies ran while one was open for 37% -> 0% of each run, Pallas kernels for 0% -> 28%
where the time goes in v1:
time: 30.7 us; the launch traced here: 30.4 us
  Pallas kernels  14.7 us (48%)
  local copies, waits for them, and re-layouts  7.42 us (24%)
  starting transfers between devices  4.62 us (15%)
  waiting for transfers between devices  3.65 us (12%)
    pallas_call x3, Pallas kernels, join(): pl.pallas_call(kernel, name='join_' + axis, out_shape=out_shape, in_specs...  10.6 us
    unnamed x12, local copies, waits for them, and re-layouts  6.12 us
    ppermute x3, starting transfers between devices, swap(): return lax.ppermute(value, (axis, 'head'), pairs)  4.62 us
    ppermute x3, waiting for transfers between devices, swap(): return lax.ppermute(value, (axis, 'head'), pairs)  3.65 us
    pallas_call x1, Pallas kernels, pick(): pl.pallas_call(kernel, name='pick', out_shape=[pltpu.VMEM((2 * count * BL...  2.11 us
    pallas_call x1, Pallas kernels, own(): pl.pallas_call(kernel, name='own', out_shape=[pltpu.VMEM((heads, rows, HD...  1.99 us
    squeeze x1, local copies, waits for them, and re-layouts, per_device(): outgoing = pick(plan, adj_mask[0, 0], border_blocks[0, 0], keys, values)  1.3 us
  transfers between devices with their start and end apart: 3, of which 1 were waited for; matrix products, arithmetic and copies ran while one was open for 0% of the time, Pallas kernels for 28%

profile of v1, /device:TPU:0, one launch (start us, length us, event | category | flops | bytes accessed | tf_op | source)
XLA Modules:
  0.0 30.4 jit_solution(8181058919457789943)
XLA Ops:
  0.0 1.3 %copy.6.border_ref = s32[2,1]{1,0:T(2,128)} copy(s32[2,1]{0,1:T(1,128)} %bitcast.15) | data formatting | bytes 16 | tf_op jit(solution)/shard_map/squeeze | solution.py:159
  1.3 2.1 %pick.1 = (bf16[256,768]{1,0:T(8,128)(2,1)S(1)}, bf16[256,768]{1,0:T(8,128)(2,1)S(1)}, bf16[256,768]{1,0:T(8,128)(2,1)S(1)}) custom-call(s32[2,2]{1,0:T(2,128)} %bitcast.14, s32[2,1]{1,0:T(2,128)} %copy.6.border_ref, bf16[256,768]{1,0:T(8,128)(2,1)} %bitcast.10, bf16[256,768]{1,0:T(8,128)(2,1)} %bitcast.12), custom_call_target="tpu_custom_call" | custom-call | tf_op jit(solution)/shard_map/pick/pallas_call | solution.py:68
  3.4 3.1 %collective-permute-start.2 = (bf16[256,768]{1,0:T(8,128)(2,1)S(1)}, bf16[256,768]{1,0:T(8,128)(2,1)}, u32[]{:S(2)}, u32[]{:S(2)}) collective-permute-start(bf16[256,768]{1,0:T(8,128)(2,1)S(1)} %get-tuple-element.16), channel_id=1, source_target_pairs={{0,4},{1,5},{4,0},{5,1},{8,12},{9,13},{12,8},{13,9},{2,6},{3,7},{6... | collective-permute-start | bytes 1179656 | tf_op jit(solution)/shard_map/ppermute | solution.py:33
  6.5 1.5 %collective-permute-start.1 = (bf16[256,768]{1,0:T(8,128)(2,1)S(1)}, bf16[256,768]{1,0:T(8,128)(2,1)}, u32[]{:S(2)}, u32[]{:S(2)}) collective-permute-start(bf16[256,768]{1,0:T(8,128)(2,1)S(1)} %get-tuple-element.15), channel_id=1, source_target_pairs={{0,2},{1,3},{2,0},{3,1},{4,6},{5,7},{6,4},{7,5},{8,10},{9,11},{10,... | collective-permute-start | bytes 1179656 | tf_op jit(solution)/shard_map/ppermute | solution.py:33
  8.0 0.0 collective-permute-start
  8.0 2.0 %own.1 = (f32[6,256,128]{2,1,0:T(8,128)S(1)}, f32[6,256,256]{2,1,0:T(8,128)S(1)}) custom-call(bf16[256,768]{1,0:T(8,128)(2,1)} %bitcast.6, bf16[256,768]{1,0:T(8,128)(2,1)} %bitcast.11, bf16[256,768]{1,0:T(8,128)(2,1)} %bitcast.13), custom_call_target="tpu_custom_call" | custom-call | flops 201326592 | bytes 1179648 | tf_op jit(solution)/shard_map/own/pallas_call | solution.py:100
  10.0 0.0 copy-start.2
  10.0 1.2 %copy-done.2 = f32[6,256,256]{2,1,0:T(8,128)} copy-done((f32[6,256,256]{2,1,0:T(8,128)}, f32[6,256,256]{2,1,0:T(8,128)S(1)}, u32[]{:S(2)}) %copy-start.2) | copy-done | bytes 1572888
  11.2 0.0 copy-start.5
  11.2 0.9 %copy-done.5 = f32[6,256,128]{2,1,0:T(8,128)} copy-done((f32[6,256,128]{2,1,0:T(8,128)}, f32[6,256,128]{2,1,0:T(8,128)S(1)}, u32[]{:S(2)}) %copy-start.5) | copy-done | bytes 786456
  12.1 3.6 %collective-permute-done.2.swapped_ref = bf16[256,768]{1,0:T(8,128)(2,1)} collective-permute-done((bf16[256,768]{1,0:T(8,128)(2,1)S(1)}, bf16[256,768]{1,0:T(8,128)(2,1)}, u32[]{:S(2)}, u32[]{:S(2)}) %collective-permute-start.2) | collective-permute-done | bytes 393248 | tf_op jit(solution)/shard_map/ppermute | solution.py:33
  15.7 3.3 %join_tm.2 = (f32[6,256,128]{2,1,0:T(8,128)S(1)}, f32[6,256,256]{2,1,0:T(8,128)S(1)}) custom-call(bf16[256,768]{1,0:T(8,128)(2,1)} %bitcast.7, bf16[256,768]{1,0:T(8,128)(2,1)} %collective-permute-done.2.swapped_ref, f32[6,256,128]{2,1,0:T(8,128)} %copy-done.5, f32[6,256,256]{2,1,0:T(8,128)} %copy-done.2), custom_call_target="tpu_custom_call" | custom-call | flops 100663296 | bytes 1179648 | tf_op jit(solution)/shard_map/join_tm/pallas_call | solution.py:144
  19.0 0.0 copy-start.1
  19.0 1.2 %copy-done.1 = f32[6,256,256]{2,1,0:T(8,128)} copy-done((f32[6,256,256]{2,1,0:T(8,128)}, f32[6,256,256]{2,1,0:T(8,128)S(1)}, u32[]{:S(2)}) %copy-start.1) | copy-done | bytes 1572888
  20.2 0.0 copy-start.4
  20.2 0.9 %copy-done.4 = f32[6,256,128]{2,1,0:T(8,128)} copy-done((f32[6,256,128]{2,1,0:T(8,128)}, f32[6,256,128]{2,1,0:T(8,128)S(1)}, u32[]{:S(2)}) %copy-start.4) | copy-done | bytes 786456
  21.1 0.0 collective-permute-done.1.swapped_ref
  21.1 3.3 %join_band.1 = (f32[6,256,128]{2,1,0:T(8,128)S(1)}, f32[6,256,256]{2,1,0:T(8,128)S(1)}) custom-call(bf16[256,768]{1,0:T(8,128)(2,1)} %bitcast.8, bf16[256,768]{1,0:T(8,128)(2,1)} %collective-permute-done.1.swapped_ref, f32[6,256,128]{2,1,0:T(8,128)} %copy-done.4, f32[6,256,256]{2,1,0:T(8,128)} %copy-done.1), custom_call_target="tpu_custom_call" | custom-call | flops 100663296 | bytes 1179648 | tf_op jit(solution)/shard_map/join_band/pallas_call | solution.py:144
  24.3 0.0 copy-start
  24.3 1.2 %copy-done = f32[6,256,256]{2,1,0:T(8,128)} copy-done((f32[6,256,256]{2,1,0:T(8,128)}, f32[6,256,256]{2,1,0:T(8,128)S(1)}, u32[]{:S(2)}) %copy-start) | copy-done | bytes 1572888
  25.5 0.0 copy-start.3
  25.5 0.9 %copy-done.3 = f32[6,256,128]{2,1,0:T(8,128)} copy-done((f32[6,256,128]{2,1,0:T(8,128)}, f32[6,256,128]{2,1,0:T(8,128)S(1)}, u32[]{:S(2)}) %copy-start.3) | copy-done | bytes 786456
  26.4 0.0 collective-permute-done.swapped_ref
  26.4 4.0 %join_tm.3 = bf16[256,768]{1,0:T(8,128)(2,1)} custom-call(bf16[256,768]{1,0:T(8,128)(2,1)} %bitcast.9, bf16[256,768]{1,0:T(8,128)(2,1)} %collective-permute-done.swapped_ref, f32[6,256,128]{2,1,0:T(8,128)} %copy-done.3, f32[6,256,256]{2,1,0:T(8,128)} %copy-done), custom_call_target="tpu_custom_call" | custom-call | flops 100663296 | bytes 1179648 | tf_op jit(solution)/shard_map/join_tm/pallas_call | solution.py:144
Async XLA Ops:
  3.4 12.3 %collective-permute-start.2 = (bf16[256,768]{1,0:T(8,128)(2,1)S(1)}, bf16[256,768]{1,0:T(8,128)(2,1)}, u32[]{:S(2)}, u32[]{:S(2)}) collective-permute-start(bf16[256,768]{1,0:T(8,128)(2,1)S(1)} %get-tuple-element.16), channel_id=1, source_target_pairs={{0,4},{1,5},{4,0},{5,1},{8,12},{9,13},{12,8},{13,9},{2,6},{3,7},{6... | collective-permute-start | bytes 1179656 | tf_op jit(solution)/shard_map/ppermute | solution.py:33
  6.5 14.6 %collective-permute-start.1 = (bf16[256,768]{1,0:T(8,128)(2,1)S(1)}, bf16[256,768]{1,0:T(8,128)(2,1)}, u32[]{:S(2)}, u32[]{:S(2)}) collective-permute-start(bf16[256,768]{1,0:T(8,128)(2,1)S(1)} %get-tuple-element.15), channel_id=1, source_target_pairs={{0,2},{1,3},{2,0},{3,1},{4,6},{5,7},{6,4},{7,5},{8,10},{9,11},{10,... | collective-permute-start | bytes 1179656 | tf_op jit(solution)/shard_map/ppermute | solution.py:33
  8.0 18.4 %collective-permute-start = (bf16[256,768]{1,0:T(8,128)(2,1)S(1)}, bf16[256,768]{1,0:T(8,128)(2,1)}, u32[]{:S(2)}, u32[]{:S(2)}) collective-permute-start(bf16[256,768]{1,0:T(8,128)(2,1)S(1)} %get-tuple-element.14), channel_id=1, source_target_pairs={{0,1},{1,0},{4,8},{5,9},{8,4},{9,5},{12,13},{13,12},{2,3},{3,2},{6... | collective-permute-start | bytes 1179656 | tf_op jit(solution)/shard_map/ppermute | solution.py:33
  10.0 1.2 %copy-start.2 = (f32[6,256,256]{2,1,0:T(8,128)}, f32[6,256,256]{2,1,0:T(8,128)S(1)}, u32[]{:S(2)}) copy-start(f32[6,256,256]{2,1,0:T(8,128)S(1)} %get-tuple-element.18.total_ref) | copy-start | bytes 4718596
  11.2 0.9 %copy-start.5 = (f32[6,256,128]{2,1,0:T(8,128)}, f32[6,256,128]{2,1,0:T(8,128)S(1)}, u32[]{:S(2)}) copy-start(f32[6,256,128]{2,1,0:T(8,128)S(1)} %get-tuple-element.17.top_ref) | copy-start | bytes 2359300
  19.0 1.2 %copy-start.1 = (f32[6,256,256]{2,1,0:T(8,128)}, f32[6,256,256]{2,1,0:T(8,128)S(1)}, u32[]{:S(2)}) copy-start(f32[6,256,256]{2,1,0:T(8,128)S(1)} %get-tuple-element.20.total_ref) | copy-start | bytes 4718596
  20.2 0.9 %copy-start.4 = (f32[6,256,128]{2,1,0:T(8,128)}, f32[6,256,128]{2,1,0:T(8,128)S(1)}, u32[]{:S(2)}) copy-start(f32[6,256,128]{2,1,0:T(8,128)S(1)} %get-tuple-element.19.top_ref) | copy-start | bytes 2359300
  24.3 1.2 %copy-start = (f32[6,256,256]{2,1,0:T(8,128)}, f32[6,256,256]{2,1,0:T(8,128)S(1)}, u32[]{:S(2)}) copy-start(f32[6,256,256]{2,1,0:T(8,128)S(1)} %get-tuple-element.22.total_ref) | copy-start | bytes 4718596
  25.5 0.9 %copy-start.3 = (f32[6,256,128]{2,1,0:T(8,128)}, f32[6,256,128]{2,1,0:T(8,128)S(1)}, u32[]{:S(2)}) copy-start(f32[6,256,128]{2,1,0:T(8,128)S(1)} %get-tuple-element.21.top_ref) | copy-start | bytes 2359300

commit v2 on v1

v2 whole, which is shorter than its diff:
```python
import itertools
import math

import jax
import jax.numpy as jnp
from jax import lax
from jax.experimental import pallas as pl
from jax.experimental.pallas import tpu as pltpu
from jax.sharding import PartitionSpec as P

BLK = 128
HD = 128
MASKED = -1e30
TO_EXP2 = math.log2(math.e) / math.sqrt(HD)
AXES = ("tm", "band", "head")
ROOM = pltpu.CompilerParams(vmem_limit_bytes=16 * 1024 * 1024)
IN_VMEM = pl.BlockSpec(memory_space=pltpu.VMEM)
ANYWHERE = pl.BlockSpec(memory_space=pl.ANY)
ROWS_BY_ROWS = (((1,), (1,)), ((), ()))
COLUMNS_BY_COLUMNS = (((0,), (0,)), ((), ()))


def swap_plan(sizes, border_count):
    steps = [(axis, phase) for axis in ("tm", "band") for phase in range(min(2, sizes[axis] - 1))]
    first, second = ("tm", 0), ("band", 0)
    if first in steps and second in steps and sizes["head"] % 2 == 0 and border_count == 1:
        rest = [step for step in steps if step not in (first, second)]
        return [(first, second)] + [(step, step) for step in rest[:1]] + [(second, first)] + [(step, step) for step in rest[1:]]
    return [(step, step) for step in steps]


def swap(value, choice):
    sizes = {axis: lax.axis_size(axis) for axis in AXES}

    def partner(place):
        axis, phase = choice[place["head"] % 2]
        there = place[axis] + 1 if place[axis] % 2 == phase else place[axis] - 1
        return {**place, axis: there} if 0 <= there < sizes[axis] else None

    def index(place):
        return (place["tm"] * sizes["band"] + place["band"]) * sizes["head"] + place["head"]

    pairs = []
    for numbers in itertools.product(*(range(sizes[axis]) for axis in AXES)):
        place = dict(zip(AXES, numbers))
        other = partner(place)
        if other is None:
            beside = {**place, "head": place["head"] ^ 1}
            if beside["head"] < sizes["head"] and partner(beside) is None:
                other = beside
        if other is not None:
            pairs.append((index(place), index(other)))
    return lax.ppermute(value, AXES, pairs)


def either(choice, function):
    even, odd = (function(*step) for step in choice)
    if choice[0] == choice[1]:
        return even
    return jnp.where(lax.rem(lax.axis_index("head"), 2) == 0, even, odd)


def goes_up(axis, phase):
    return lax.rem(lax.axis_index(axis), 2) == phase


def has_partner(axis, phase):
    here, size = lax.axis_index(axis), lax.axis_size(axis)
    return jnp.where(goes_up(axis, phase), jnp.where(here < size - 1, 1, 0), jnp.where(here > 0, 1, 0))


def pick(plan, adj_mask, border_blocks, keys, values):
    width = keys.shape[1]
    blocks = adj_mask.shape[1]
    counts = [border_blocks.shape[0] if choice[0][0] == "band" else 1 for choice in plan]

    def kernel(adj_hbm, border_hbm, key_hbm, value_hbm, *rest):
        outs, (adj_ref, border_ref, key_ref, value_ref, sems) = rest[: len(plan)], rest[len(plan) :]
        pairs = ((adj_hbm, adj_ref), (border_hbm, border_ref), (key_hbm, key_ref), (value_hbm, value_ref))
        copies = [pltpu.make_async_copy(*pair, sems.at[number]) for number, pair in enumerate(pairs)]
        for copy in copies:
            copy.start()
        for copy in copies:
            copy.wait()
        for out, choice, count in zip(outs, plan, counts):
            for entry in range(count):

                def block(axis, phase):
                    up = goes_up(axis, phase)
                    if axis == "band":
                        return border_ref[entry, jnp.where(up, 1, 0)]
                    row = jnp.where(up, 0, 1)
                    return sum(number * adj_ref[row, number] for number in range(1, blocks))

                rows = pl.ds(pl.multiple_of(either(choice, block) * BLK, BLK), BLK)
                out[pl.ds(entry * BLK, BLK)] = key_ref[rows]
                out[pl.ds((count + entry) * BLK, BLK)] = value_ref[rows]

    arrays = (adj_mask, border_blocks, keys, values)
    return pl.pallas_call(
        kernel,
        name="pick",
        compiler_params=ROOM,
        out_shape=[pltpu.VMEM((2 * count * BLK, width), keys.dtype) for count in counts],
        in_specs=[ANYWHERE] * 4,
        out_specs=[IN_VMEM] * len(plan),
        scratch_shapes=[pltpu.SMEM(array.shape, array.dtype) for array in arrays[:2]]
        + [pltpu.VMEM(array.shape, array.dtype) for array in arrays[2:]]
        + [pltpu.SemaphoreType.DMA((4,))],
    )(*(pltpu.with_memory_space_constraint(array, pltpu.HBM) for array in arrays))


def score(key, query):
    return lax.dot_general(key, query, ROWS_BY_ROWS, preferred_element_type=jnp.float32) * TO_EXP2


def weigh(value, weights):
    return lax.dot_general(value, weights, COLUMNS_BY_COLUMNS, preferred_element_type=jnp.float32)


def state_shapes(heads, rows):
    return [pltpu.VMEM((heads, height, rows), jnp.float32) for height in (1, 1, HD)]


def cost(rows, keys, width):
    return pl.CostEstimate(
        flops=4 * rows * keys * width, bytes_accessed=2 * (rows + 2 * keys) * width, transcendentals=rows * keys * (width // HD)
    )


def own(queries, keys, values):
    rows, width = queries.shape
    heads = width // HD

    def kernel(query_ref, key_ref, value_ref, top_ref, total_ref, part_ref):
        for head in range(heads):
            cols = slice(head * HD, (head + 1) * HD)
            scores = score(key_ref[:, cols], query_ref[:, cols])
            top = jnp.max(scores, axis=0, keepdims=True)
            weights = jnp.exp2(scores - top)
            top_ref[head] = top
            total_ref[head] = jnp.sum(weights, axis=0, keepdims=True)
            part_ref[head] = weigh(value_ref[:, cols], weights.astype(value_ref.dtype))

    return pl.pallas_call(
        kernel,
        name="own",
        compiler_params=ROOM,
        out_shape=state_shapes(heads, rows),
        in_specs=[IN_VMEM] * 3,
        out_specs=[IN_VMEM] * 3,
        cost_estimate=cost(rows, keys.shape[0], width),
    )(queries, keys, values)


def join(queries, sources, choices, state, last):
    rows, width = queries.shape
    heads = width // HD
    lengths = [source.shape[0] // 2 for source in sources]

    def kernel(query_ref, *rest):
        source_refs, (top_ref, total_ref, part_ref), outs = rest[: len(sources)], rest[len(sources) :][:3], rest[len(sources) + 3 :]
        biases = [jnp.where(either(choice, has_partner) == 1, 0.0, MASKED).astype(jnp.float32) for choice in choices]
        columns = [slice(head * HD, (head + 1) * HD) for head in range(heads)]
        scores = [
            [score(ref[:length, cols], query_ref[:, cols]) for ref, length in zip(source_refs, lengths)] for cols in columns
        ]
        softened = []
        for head in range(heads):
            before = top_ref[head]
            top = before
            for part, bias in zip(scores[head], biases):
                top = jnp.maximum(top, jnp.max(part, axis=0, keepdims=True) + bias)
            weights = [jnp.exp2(part - (top - bias)) for part, bias in zip(scores[head], biases)]
            kept = jnp.exp2(before - top)
            total = total_ref[head] * kept
            for part in weights:
                total = total + jnp.sum(part, axis=0, keepdims=True)
            softened.append((top, kept, total, jnp.concatenate([part.astype(query_ref.dtype) for part in weights])))
        parts = [
            weigh(jnp.concatenate([ref[length:, cols] for ref, length in zip(source_refs, lengths)]), softened[head][3])
            for head, cols in enumerate(columns)
        ]
        copies = []
        for head, cols in enumerate(columns):
            top, kept, total, _ = softened[head]
            part = part_ref[head] * kept + parts[head]
            if last:
                out_hbm, out_ref, sems = outs
                out_ref[head] = (part * (1.0 / total)).astype(out_ref.dtype).T
                copies.append(pltpu.make_async_copy(out_ref.at[head], out_hbm.at[:, cols], sems.at[head]))
                copies[-1].start()
            else:
                outs[0][head], outs[1][head], outs[2][head] = top, total, part
        for copy in copies:
            copy.wait()

    operands = [pltpu.with_memory_space_constraint(array, pltpu.VMEM) for array in (queries, *sources, *state)]
    return pl.pallas_call(
        kernel,
        name="finish" if last else "join",
        compiler_params=ROOM,
        out_shape=pltpu.HBM((rows, width), queries.dtype) if last else state_shapes(heads, rows),
        in_specs=[IN_VMEM] * len(operands),
        out_specs=ANYWHERE if last else [IN_VMEM] * 3,
        scratch_shapes=[pltpu.VMEM((heads, rows, HD), queries.dtype), pltpu.SemaphoreType.DMA((heads,))] if last else [],
        cost_estimate=cost(rows, sum(lengths), width),
    )(*operands)


def per_device(queries, keys, values, adj_mask, border_blocks):
    queries, keys, values = queries[0, 0], keys[0, 0], values[0, 0]
    border_blocks = border_blocks[0, 0].T
    plan = swap_plan({axis: lax.axis_size(axis) for axis in AXES}, border_blocks.shape[0])
    outgoing = pick(plan, adj_mask[0, 0], border_blocks, keys, values)
    incoming = [swap(rows, choice) for rows, choice in zip(outgoing, plan)]
    state = own(queries, keys, values)
    cut = max(0, len(plan) - 2)
    for number in range(cut):
        state = join(queries, incoming[number : number + 1], plan[number : number + 1], state, False)
    return join(queries, incoming[cut:], plan[cut:], state, True)[None, None]


def solution(mesh):
    wide = P(("clip", "tm"), "band", None, "head")
    narrow = P(("clip", "tm"), "band", None, None)
    return jax.shard_map(
        per_device, mesh=mesh, in_specs=(wide, wide, wide, narrow, narrow), out_specs=wide, check_vma=False
    )
```

time: 30.7 us -> 15.7 us (0.51)
  the two profiles are of different devices: /device:TPU:0 before, /device:TPU:30 now
where the time goes in v2:
time: 15.7 us; the launch traced here: 15.5 us
  waiting for transfers between devices  7.53 us (48%)
  Pallas kernels  5.26 us (34%)
  starting transfers between devices  1.65 us (11%)
  local copies, waits for them, and re-layouts  1 us (6%)
    ppermute x3, waiting for transfers between devices, swap(): return lax.ppermute(value, AXES, pairs)  7.53 us
    pallas_call x2, Pallas kernels, join(): pl.pallas_call(kernel, name='finish' if last else 'join', compiler_params...  2.1 us
    pallas_call x1, Pallas kernels, own(): pl.pallas_call(kernel, name='own', compiler_params=ROOM, out_shape=state_...  1.86 us
    ppermute x3, starting transfers between devices, swap(): return lax.ppermute(value, AXES, pairs)  1.65 us
    pallas_call x1, Pallas kernels, pick(): pl.pallas_call(kernel, name='pick', compiler_params=ROOM, out_shape=[pltp...  1.3 us
    unnamed x6, local copies, waits for them, and re-layouts  1 us
  transfers between devices with their start and end apart: 3, of which 1 were waited for; matrix products, arithmetic and copies ran while one was open for 0% of the time, Pallas kernels for 16%

profile of v2, /device:TPU:30, one launch (start us, length us, event | category | flops | bytes accessed | tf_op | source)
XLA Modules:
  0.0 15.5 jit_solution(8928161016945892979)
XLA Ops:
  0.0 0.0 copy-start
  0.0 0.0 copy-start.1
  0.0 1.3 %pick.1 = (bf16[256,768]{1,0:T(8,128)(2,1)S(1)}, bf16[256,768]{1,0:T(8,128)(2,1)S(1)}, bf16[256,768]{1,0:T(8,128)(2,1)S(1)}) custom-call(s32[2,2]{1,0:T(2,128)} %bitcast.13, s32[1,2]{1,0:T(1,128)} %bitcast.14, bf16[256,768]{1,0:T(8,128)(2,1)} %bitcast.9, bf16[256,768]{1,0:T(8,128)(2,1)} %bitcast.11), custom_call_target="tpu_custom_call" | custom-call | tf_op jit(solution)/shard_map/pick/pallas_call | solution.py:100
  1.3 0.5 %collective-permute-start.2 = (bf16[256,768]{1,0:T(8,128)(2,1)S(1)}, bf16[256,768]{1,0:T(8,128)(2,1)S(1)}, u32[]{:S(2)}, u32[]{:S(2)}) collective-permute-start(bf16[256,768]{1,0:T(8,128)(2,1)S(1)} %get-tuple-element.16), channel_id=1, source_target_pairs={{0,4},{1,3},{2,6},{3,1},{4,0},{5,7},{6,2},{7,5},{8,12},{9,11},{10,... | collective-permute-start | bytes 1179656 | tf_op jit(solution)/shard_map/ppermute | solution.py:53
  1.8 0.0 collective-permute-start
  1.8 1.1 %collective-permute-start.1 = (bf16[256,768]{1,0:T(8,128)(2,1)S(1)}, bf16[256,768]{1,0:T(8,128)(2,1)S(1)}, u32[]{:S(2)}, u32[]{:S(2)}) collective-permute-start(bf16[256,768]{1,0:T(8,128)(2,1)S(1)} %get-tuple-element.15), channel_id=1, source_target_pairs={{0,2},{1,5},{2,0},{3,7},{4,6},{5,1},{6,4},{7,3},{8,10},{9,13},{10,... | collective-permute-start | bytes 1179656 | tf_op jit(solution)/shard_map/ppermute | solution.py:53
  3.0 0.0 copy-done
  3.0 0.0 copy-done.1
  3.0 0.0 copy-start.2
  3.0 1.0 %copy-done.2 = bf16[1,1,256,768]{3,2,1,0:T(8,128)(2,1)S(1)} copy-done((bf16[1,1,256,768]{3,2,1,0:T(8,128)(2,1)S(1)}, bf16[1,1,256,768]{3,2,1,0:T(8,128)(2,1)}, u32[]{:S(2)}) %copy-start.2) | copy-done | bytes 393240
  4.0 1.9 %own.1 = (f32[6,1,256]{2,1,0:T(1,128)S(1)}, f32[6,1,256]{2,1,0:T(1,128)S(1)}, f32[6,128,256]{2,1,0:T(8,128)S(1)}) custom-call(bf16[256,768]{1,0:T(8,128)(2,1)S(1)} %bitcast.6, bf16[256,768]{1,0:T(8,128)(2,1)S(1)} %bitcast.10, bf16[256,768]{1,0:T(8,128)(2,1)S(1)} %bitcast.12), custom_call_target="tpu_custom_call" | custom-call | flops 201326592 | bytes 1179648 | tf_op jit(solution)/shard_map/own/pallas_call | solution.py:145
  5.8 7.5 %collective-permute-done.2.rest_0_ = bf16[256,768]{1,0:T(8,128)(2,1)S(1)} collective-permute-done((bf16[256,768]{1,0:T(8,128)(2,1)S(1)}, bf16[256,768]{1,0:T(8,128)(2,1)S(1)}, u32[]{:S(2)}, u32[]{:S(2)}) %collective-permute-start.2) | collective-permute-done | bytes 393248 | tf_op jit(solution)/shard_map/ppermute | solution.py:53
  13.4 0.6 %join.1 = (f32[6,1,256]{2,1,0:T(1,128)S(1)}, f32[6,1,256]{2,1,0:T(1,128)S(1)}, f32[6,128,256]{2,1,0:T(8,128)S(1)}) custom-call(bf16[256,768]{1,0:T(8,128)(2,1)S(1)} %bitcast.7, bf16[256,768]{1,0:T(8,128)(2,1)S(1)} %collective-permute-done.2.rest_0_, f32[6,1,256]{2,1,0:T(1,128)S(1)} %get-tuple-element.17.rest_1_, f32[6,1,256]{2,1,0:T(1,128)S(1)} %get-tuple-element.18.rest_2_, ...), custom_call_target="tpu_custom_call" | custom-call | flops 100663296 | bytes 786432 | tf_op jit(solution)/shard_map/join/pallas_call | solution.py:199
  13.9 0.0 collective-permute-done.rest_0_
  13.9 0.0 collective-permute-done.1.rest_1_
  14.0 1.5 %finish.1 = bf16[256,768]{1,0:T(8,128)(2,1)} custom-call(bf16[256,768]{1,0:T(8,128)(2,1)S(1)} %bitcast.8, bf16[256,768]{1,0:T(8,128)(2,1)S(1)} %collective-permute-done.rest_0_, bf16[256,768]{1,0:T(8,128)(2,1)S(1)} %collective-permute-done.1.rest_1_, f32[6,1,256]{2,1,0:T(1,128)S(1)} %get-tuple-element.20.rest_2_, ...), custom_call_target="tpu_custom_call" | custom-call | flops 201326592 | bytes 1179648 | tf_op jit(solution)/shard_map/finish/pallas_call | solution.py:199
Async XLA Ops:
  0.0 3.0 %copy-start = (bf16[1,1,256,768]{3,2,1,0:T(8,128)(2,1)S(1)}, bf16[1,1,256,768]{3,2,1,0:T(8,128)(2,1)}, u32[]{:S(2)}) copy-start(bf16[1,1,256,768]{3,2,1,0:T(8,128)(2,1)} %param.5) | copy-start | bytes 1179652
  0.0 3.0 %copy-start.1 = (bf16[1,1,256,768]{3,2,1,0:T(8,128)(2,1)S(1)}, bf16[1,1,256,768]{3,2,1,0:T(8,128)(2,1)}, u32[]{:S(2)}) copy-start(bf16[1,1,256,768]{3,2,1,0:T(8,128)(2,1)} %param.6) | copy-start | bytes 1179652
  1.3 12.0 %collective-permute-start.2 = (bf16[256,768]{1,0:T(8,128)(2,1)S(1)}, bf16[256,768]{1,0:T(8,128)(2,1)S(1)}, u32[]{:S(2)}, u32[]{:S(2)}) collective-permute-start(bf16[256,768]{1,0:T(8,128)(2,1)S(1)} %get-tuple-element.16), channel_id=1, source_target_pairs={{0,4},{1,3},{2,6},{3,1},{4,0},{5,7},{6,2},{7,5},{8,12},{9,11},{10,... | collective-permute-start | bytes 1179656 | tf_op jit(solution)/shard_map/ppermute | solution.py:53
  1.8 12.1 %collective-permute-start = (bf16[256,768]{1,0:T(8,128)(2,1)S(1)}, bf16[256,768]{1,0:T(8,128)(2,1)S(1)}, u32[]{:S(2)}, u32[]{:S(2)}) collective-permute-start(bf16[256,768]{1,0:T(8,128)(2,1)S(1)} %get-tuple-element.14), channel_id=1, source_target_pairs={{0,1},{1,0},{2,3},{3,2},{4,8},{5,9},{6,10},{7,11},{8,4},{9,5},{10,... | collective-permute-start | bytes 1179656 | tf_op jit(solution)/shard_map/ppermute | solution.py:53
  1.8 12.1 %collective-permute-start.1 = (bf16[256,768]{1,0:T(8,128)(2,1)S(1)}, bf16[256,768]{1,0:T(8,128)(2,1)S(1)}, u32[]{:S(2)}, u32[]{:S(2)}) collective-permute-start(bf16[256,768]{1,0:T(8,128)(2,1)S(1)} %get-tuple-element.15), channel_id=1, source_target_pairs={{0,2},{1,5},{2,0},{3,7},{4,6},{5,1},{6,4},{7,3},{8,10},{9,13},{10,... | collective-permute-start | bytes 1179656 | tf_op jit(solution)/shard_map/ppermute | solution.py:53
  3.0 1.0 %copy-start.2 = (bf16[1,1,256,768]{3,2,1,0:T(8,128)(2,1)S(1)}, bf16[1,1,256,768]{3,2,1,0:T(8,128)(2,1)}, u32[]{:S(2)}) copy-start(bf16[1,1,256,768]{3,2,1,0:T(8,128)(2,1)} %param.7) | copy-start | bytes 1179652

commit v3 on v2

--- a/solution.py
+++ b/solution.py
@@ -75,13 +75,14 @@
     counts = [border_blocks.shape[0] if choice[0][0] == "band" else 1 for choice in plan]
 
     def kernel(adj_hbm, border_hbm, key_hbm, value_hbm, *rest):
-        outs, (adj_ref, border_ref, key_ref, value_ref, sems) = rest[: len(plan)], rest[len(plan) :]
+        outs, (key_ref, value_ref, adj_ref, border_ref, sems) = rest[: len(plan)], rest[len(plan) :]
         pairs = ((adj_hbm, adj_ref), (border_hbm, border_ref), (key_hbm, key_ref), (value_hbm, value_ref))
         copies = [pltpu.make_async_copy(*pair, sems.at[number]) for number, pair in enumerate(pairs)]
         for copy in copies:
             copy.start()
-        for copy in copies:
+        for copy in copies[:2]:
             copy.wait()
+        chosen = []
         for out, choice, count in zip(outs, plan, counts):
             for entry in range(count):
 
@@ -93,20 +94,24 @@
                     return sum(number * adj_ref[row, number] for number in range(1, blocks))
 
                 rows = pl.ds(pl.multiple_of(either(choice, block) * BLK, BLK), BLK)
-                out[pl.ds(entry * BLK, BLK)] = key_ref[rows]
-                out[pl.ds((count + entry) * BLK, BLK)] = value_ref[rows]
+                chosen.append((out, rows, entry * BLK, (count + entry) * BLK))
+        copies[2].wait()
+        for out, rows, place, _ in chosen:
+            out[pl.ds(place, BLK)] = key_ref[rows]
+        copies[3].wait()
+        for out, rows, _, place in chosen:
+            out[pl.ds(place, BLK)] = value_ref[rows]
 
     arrays = (adj_mask, border_blocks, keys, values)
     return pl.pallas_call(
         kernel,
         name="pick",
         compiler_params=ROOM,
-        out_shape=[pltpu.VMEM((2 * count * BLK, width), keys.dtype) for count in counts],
+        out_shape=[pltpu.VMEM((2 * count * BLK, width), keys.dtype) for count in counts]
+        + [pltpu.VMEM(array.shape, array.dtype) for array in arrays[2:]],
         in_specs=[ANYWHERE] * 4,
-        out_specs=[IN_VMEM] * len(plan),
-        scratch_shapes=[pltpu.SMEM(array.shape, array.dtype) for array in arrays[:2]]
-        + [pltpu.VMEM(array.shape, array.dtype) for array in arrays[2:]]
-        + [pltpu.SemaphoreType.DMA((4,))],
+        out_specs=[IN_VMEM] * (len(plan) + 2),
+        scratch_shapes=[pltpu.SMEM(array.shape, array.dtype) for array in arrays[:2]] + [pltpu.SemaphoreType.DMA((4,))],
     )(*(pltpu.with_memory_space_constraint(array, pltpu.HBM) for array in arrays))
 
 
@@ -133,14 +138,17 @@
     heads = width // HD
 
     def kernel(query_ref, key_ref, value_ref, top_ref, total_ref, part_ref):
+        columns = [slice(head * HD, (head + 1) * HD) for head in range(heads)]
+        scores = [score(key_ref[:, cols], query_ref[:, cols]) for cols in columns]
+        rounded = []
         for head in range(heads):
-            cols = slice(head * HD, (head + 1) * HD)
-            scores = score(key_ref[:, cols], query_ref[:, cols])
-            top = jnp.max(scores, axis=0, keepdims=True)
-            weights = jnp.exp2(scores - top)
+            top = jnp.max(scores[head], axis=0, keepdims=True)
+            weights = jnp.exp2(scores[head] - top)
             top_ref[head] = top
             total_ref[head] = jnp.sum(weights, axis=0, keepdims=True)
-            part_ref[head] = weigh(value_ref[:, cols], weights.astype(value_ref.dtype))
+            rounded.append(weights.astype(value_ref.dtype))
+        for head, cols in enumerate(columns):
+            part_ref[head] = weigh(value_ref[:, cols], rounded[head])
 
     return pl.pallas_call(
         kernel,
@@ -149,8 +157,8 @@
         out_shape=state_shapes(heads, rows),
         in_specs=[IN_VMEM] * 3,
         out_specs=[IN_VMEM] * 3,
-        cost_estimate=cost(rows, keys.shape[0], width),
-    )(queries, keys, values)
+
+    )(*(pltpu.with_memory_space_constraint(array, pltpu.VMEM) for array in (queries, keys, values)))
 
 
 def join(queries, sources, choices, state, last):
@@ -212,9 +220,11 @@
     queries, keys, values = queries[0, 0], keys[0, 0], values[0, 0]
     border_blocks = border_blocks[0, 0].T
     plan = swap_plan({axis: lax.axis_size(axis) for axis in AXES}, border_blocks.shape[0])
-    outgoing = pick(plan, adj_mask[0, 0], border_blocks, keys, values)
+    *outgoing, keys, values = pick(plan, adj_mask[0, 0], border_blocks, keys, values)
+    state = own(queries, keys, values)
+    for number in range(2, len(plan)):
+        outgoing[number], state = lax.optimization_barrier((outgoing[number], state))
     incoming = [swap(rows, choice) for rows, choice in zip(outgoing, plan)]
-    state = own(queries, keys, values)
     cut = max(0, len(plan) - 2)
     for number in range(cut):
         state = join(queries, incoming[number : number + 1], plan[number : number + 1], state, False)

time: 15.7 us -> 15.3 us (0.975)
  the two profiles are of different devices: /device:TPU:30 before, /device:TPU:1 now
where the time goes in v3:
time: 15.3 us; the launch traced here: 15.2 us
  waiting for transfers between devices  6.29 us (41%)
  starting transfers between devices  4.76 us (31%)
  Pallas kernels  4.12 us (27%)
    ppermute x3, waiting for transfers between devices, swap(): return lax.ppermute(value, AXES, pairs)  6.29 us
    ppermute x3, starting transfers between devices, swap(): return lax.ppermute(value, AXES, pairs)  4.76 us
    pallas_call x2, Pallas kernels, join(): pl.pallas_call(kernel, name='finish' if last else 'join', compiler_params...  2.09 us
    pallas_call x1, Pallas kernels, pick(): pl.pallas_call(kernel, name='pick', compiler_params=ROOM, out_shape=[pltp...  1.24 us
    pallas_call x1, Pallas kernels, own(): pl.pallas_call(kernel, name='own', compiler_params=ROOM, out_shape=state_...  0.79 us
  transfers between devices with their start and end apart: 3, of which 2 were waited for; matrix products, arithmetic and copies ran while one was open for 0% of the time, Pallas kernels for 9%

profile of v3, /device:TPU:1, one launch (start us, length us, event | category | flops | bytes accessed | tf_op | source)
XLA Modules:
  0.0 15.2 jit_solution(10364854878739384488)
XLA Ops:
  0.0 0.0 copy-start
  0.0 1.2 %pick.1 = (bf16[256,768]{1,0:T(8,128)(2,1)S(1)}, bf16[256,768]{1,0:T(8,128)(2,1)S(1)}, bf16[256,768]{1,0:T(8,128)(2,1)S(1)}, bf16[256,768]{1,0:T(8,128)(2,1)S(1)}, bf16[256,768]{1,0:T(8,128)(2,1)S(1)}) custom-call(s32[2,2]{1,0:T(2,128)} %bitcast.11, s32[1,2]{1,0:T(1,128)} %bitcast.12, bf16[256,768]{1,0:T(8,128)(2,1)} %bitcast.9, bf16[256,768]{1,0:T(8,128)(2,1)} %bitcast.10), custom_call_target="tpu_custom_call" | custom-call | tf_op jit(solution)/shard_map/pick/pallas_call | solution.py:106
  1.2 2.1 %collective-permute-start.2 = (bf16[256,768]{1,0:T(8,128)(2,1)S(1)}, bf16[256,768]{1,0:T(8,128)(2,1)S(1)}, u32[]{:S(2)}, u32[]{:S(2)}) collective-permute-start(bf16[256,768]{1,0:T(8,128)(2,1)S(1)} %get-tuple-element.28), channel_id=1, source_target_pairs={{0,4},{1,3},{2,6},{3,1},{4,0},{5,7},{6,2},{7,5},{8,12},{9,11},{10,... | collective-permute-start | bytes 1179656 | tf_op jit(solution)/shard_map/ppermute | solution.py:53
  3.4 1.0 %collective-permute-start = (bf16[256,768]{1,0:T(8,128)(2,1)S(1)}, bf16[256,768]{1,0:T(8,128)(2,1)S(1)}, u32[]{:S(2)}, u32[]{:S(2)}) collective-permute-start(bf16[256,768]{1,0:T(8,128)(2,1)S(1)} %get-tuple-element.20), channel_id=1, source_target_pairs={{0,1},{1,0},{2,3},{3,2},{4,8},{5,9},{6,10},{7,11},{8,4},{9,5},{10,... | collective-permute-start | bytes 1179656 | tf_op jit(solution)/shard_map/ppermute | solution.py:53
  4.4 0.0 copy-done
  4.4 0.8 %own.1 = (f32[6,1,256]{2,1,0:T(1,128)S(1)}, f32[6,1,256]{2,1,0:T(1,128)S(1)}, f32[6,128,256]{2,1,0:T(8,128)S(1)}) custom-call(bf16[256,768]{1,0:T(8,128)(2,1)S(1)} %bitcast.6, bf16[256,768]{1,0:T(8,128)(2,1)S(1)} %get-tuple-element.22.key_ref, bf16[256,768]{1,0:T(8,128)(2,1)S(1)} %get-tuple-element.23.value_ref), custom_call_target="tpu_custom_call" | custom-call | tf_op jit(solution)/shard_map/own/pallas_call | solution.py:153
  5.2 1.6 %collective-permute-start.1 = (bf16[256,768]{1,0:T(8,128)(2,1)S(1)}, bf16[256,768]{1,0:T(8,128)(2,1)S(1)}, u32[]{:S(2)}, u32[]{:S(2)}) collective-permute-start(bf16[256,768]{1,0:T(8,128)(2,1)S(1)} %get-tuple-element.27), channel_id=1, source_target_pairs={{0,2},{1,5},{2,0},{3,7},{4,6},{5,1},{6,4},{7,3},{8,10},{9,13},{10,... | collective-permute-start | bytes 1179656 | tf_op jit(solution)/shard_map/ppermute | solution.py:53
  6.8 2.3 %collective-permute-done.2.rest_0_ = bf16[256,768]{1,0:T(8,128)(2,1)S(1)} collective-permute-done((bf16[256,768]{1,0:T(8,128)(2,1)S(1)}, bf16[256,768]{1,0:T(8,128)(2,1)S(1)}, u32[]{:S(2)}, u32[]{:S(2)}) %collective-permute-start.2) | collective-permute-done | bytes 393248 | tf_op jit(solution)/shard_map/ppermute | solution.py:53
  9.1 0.6 %join.1 = (f32[6,1,256]{2,1,0:T(1,128)S(1)}, f32[6,1,256]{2,1,0:T(1,128)S(1)}, f32[6,128,256]{2,1,0:T(8,128)S(1)}) custom-call(bf16[256,768]{1,0:T(8,128)(2,1)S(1)} %bitcast.7, bf16[256,768]{1,0:T(8,128)(2,1)S(1)} %collective-permute-done.2.rest_0_, f32[6,1,256]{2,1,0:T(1,128)S(1)} %get-tuple-element.29.rest_1_, f32[6,1,256]{2,1,0:T(1,128)S(1)} %get-tuple-element.30.rest_2_, ...), custom_call_target="tpu_custom_call" | custom-call | flops 100663296 | bytes 786432 | tf_op jit(solution)/shard_map/join/pallas_call | solution.py:207
  9.7 0.0 collective-permute-done.rest_0_
  9.7 4.0 %collective-permute-done.1.rest_1_ = bf16[256,768]{1,0:T(8,128)(2,1)S(1)} collective-permute-done((bf16[256,768]{1,0:T(8,128)(2,1)S(1)}, bf16[256,768]{1,0:T(8,128)(2,1)S(1)}, u32[]{:S(2)}, u32[]{:S(2)}) %collective-permute-start.1) | collective-permute-done | bytes 393248 | tf_op jit(solution)/shard_map/ppermute | solution.py:53
  13.7 1.5 %finish.1 = bf16[256,768]{1,0:T(8,128)(2,1)} custom-call(bf16[256,768]{1,0:T(8,128)(2,1)S(1)} %bitcast.8, bf16[256,768]{1,0:T(8,128)(2,1)S(1)} %collective-permute-done.rest_0_, bf16[256,768]{1,0:T(8,128)(2,1)S(1)} %collective-permute-done.1.rest_1_, f32[6,1,256]{2,1,0:T(1,128)S(1)} %get-tuple-element.32.rest_2_, ...), custom_call_target="tpu_custom_call" | custom-call | flops 201326592 | bytes 1179648 | tf_op jit(solution)/shard_map/finish/pallas_call | solution.py:207
Async XLA Ops:
  0.0 4.4 %copy-start = (bf16[1,1,256,768]{3,2,1,0:T(8,128)(2,1)S(1)}, bf16[1,1,256,768]{3,2,1,0:T(8,128)(2,1)}, u32[]{:S(2)}) copy-start(bf16[1,1,256,768]{3,2,1,0:T(8,128)(2,1)} %param.5) | copy-start | bytes 1179652
  1.2 7.9 %collective-permute-start.2 = (bf16[256,768]{1,0:T(8,128)(2,1)S(1)}, bf16[256,768]{1,0:T(8,128)(2,1)S(1)}, u32[]{:S(2)}, u32[]{:S(2)}) collective-permute-start(bf16[256,768]{1,0:T(8,128)(2,1)S(1)} %get-tuple-element.28), channel_id=1, source_target_pairs={{0,4},{1,3},{2,6},{3,1},{4,0},{5,7},{6,2},{7,5},{8,12},{9,11},{10,... | collective-permute-start | bytes 1179656 | tf_op jit(solution)/shard_map/ppermute | solution.py:53
  3.4 6.4 %collective-permute-start = (bf16[256,768]{1,0:T(8,128)(2,1)S(1)}, bf16[256,768]{1,0:T(8,128)(2,1)S(1)}, u32[]{:S(2)}, u32[]{:S(2)}) collective-permute-start(bf16[256,768]{1,0:T(8,128)(2,1)S(1)} %get-tuple-element.20), channel_id=1, source_target_pairs={{0,1},{1,0},{2,3},{3,2},{4,8},{5,9},{6,10},{7,11},{8,4},{9,5},{10,... | collective-permute-start | bytes 1179656 | tf_op jit(solution)/shard_map/ppermute | solution.py:53
  5.2 8.5 %collective-permute-start.1 = (bf16[256,768]{1,0:T(8,128)(2,1)S(1)}, bf16[256,768]{1,0:T(8,128)(2,1)S(1)}, u32[]{:S(2)}, u32[]{:S(2)}) collective-permute-start(bf16[256,768]{1,0:T(8,128)(2,1)S(1)} %get-tuple-element.27), channel_id=1, source_target_pairs={{0,2},{1,5},{2,0},{3,7},{4,6},{5,1},{6,4},{7,3},{8,10},{9,13},{10,... | collective-permute-start | bytes 1179656 | tf_op jit(solution)/shard_map/ppermute | solution.py:53

commit v4 on v3

--- a/solution.py
+++ b/solution.py
@@ -1,3 +1,4 @@
+import functools
 import itertools
 import math
 
@@ -11,6 +12,7 @@
 BLK = 128
 HD = 128
 MASKED = -1e30
+SAFE_TOTAL = 2.0**90
 TO_EXP2 = math.log2(math.e) / math.sqrt(HD)
 AXES = ("tm", "band", "head")
 ROOM = pltpu.CompilerParams(vmem_limit_bytes=16 * 1024 * 1024)
@@ -161,57 +163,96 @@
     )(*(pltpu.with_memory_space_constraint(array, pltpu.VMEM) for array in (queries, keys, values)))
 
 
-def join(queries, sources, choices, state, last):
+def split(refs, lengths, cols, values):
+    return [ref[length:, cols] if values else ref[:length, cols] for ref, length in zip(refs, lengths)]
+
+
+def join(queries, source, choice, state):
     rows, width = queries.shape
     heads = width // HD
+    length = source.shape[0] // 2
+
+    def kernel(query_ref, source_ref, top_ref, total_ref, part_ref, new_top_ref, new_total_ref, new_part_ref):
+        bias = jnp.where(either(choice, has_partner) == 1, 0.0, MASKED).astype(jnp.float32)
+        columns = [slice(head * HD, (head + 1) * HD) for head in range(heads)]
+        scores = [score(source_ref[:length, cols], query_ref[:, cols]) for cols in columns]
+        rounded, kept = [], []
+        for head in range(heads):
+            top = jnp.maximum(top_ref[head], jnp.max(scores[head], axis=0, keepdims=True) + bias)
+            weights = jnp.exp2(scores[head] - (top - bias))
+            kept.append(jnp.exp2(top_ref[head] - top))
+            new_top_ref[head] = top
+            new_total_ref[head] = total_ref[head] * kept[head] + jnp.sum(weights, axis=0, keepdims=True)
+            rounded.append(weights.astype(query_ref.dtype))
+        for head, cols in enumerate(columns):
+            new_part_ref[head] = part_ref[head] * kept[head] + weigh(source_ref[length:, cols], rounded[head])
+
+    operands = [pltpu.with_memory_space_constraint(array, pltpu.VMEM) for array in (queries, source, *state)]
+    return pl.pallas_call(
+        kernel,
+        name="join",
+        compiler_params=ROOM,
+        out_shape=state_shapes(heads, rows),
+        in_specs=[IN_VMEM] * len(operands),
+        out_specs=[IN_VMEM] * 3,
+        cost_estimate=cost(rows, length, width),
+    )(*operands)
+
+
+def finish(queries, sources, choices, state):
+    rows, width = queries.shape
+    heads = width // HD
+    count = len(sources)
     lengths = [source.shape[0] // 2 for source in sources]
 
     def kernel(query_ref, *rest):
-        source_refs, (top_ref, total_ref, part_ref), outs = rest[: len(sources)], rest[len(sources) :][:3], rest[len(sources) + 3 :]
+        source_refs, (top_ref, total_ref, part_ref, out_hbm, out_ref, sems) = rest[:count], rest[count:]
         biases = [jnp.where(either(choice, has_partner) == 1, 0.0, MASKED).astype(jnp.float32) for choice in choices]
         columns = [slice(head * HD, (head + 1) * HD) for head in range(heads)]
-        scores = [
-            [score(ref[:length, cols], query_ref[:, cols]) for ref, length in zip(source_refs, lengths)] for cols in columns
-        ]
-        softened = []
-        for head in range(heads):
-            before = top_ref[head]
-            top = before
-            for part, bias in zip(scores[head], biases):
-                top = jnp.maximum(top, jnp.max(part, axis=0, keepdims=True) + bias)
-            weights = [jnp.exp2(part - (top - bias)) for part, bias in zip(scores[head], biases)]
-            kept = jnp.exp2(before - top)
-            total = total_ref[head] * kept
-            for part in weights:
-                total = total + jnp.sum(part, axis=0, keepdims=True)
-            softened.append((top, kept, total, jnp.concatenate([part.astype(query_ref.dtype) for part in weights])))
-        parts = [
-            weigh(jnp.concatenate([ref[length:, cols] for ref, length in zip(source_refs, lengths)]), softened[head][3])
-            for head, cols in enumerate(columns)
-        ]
-        copies = []
-        for head, cols in enumerate(columns):
-            top, kept, total, _ = softened[head]
-            part = part_ref[head] * kept + parts[head]
-            if last:
-                out_hbm, out_ref, sems = outs
-                out_ref[head] = (part * (1.0 / total)).astype(out_ref.dtype).T
+
+        def run(true_maximum):
+            scores = [[score(key, query_ref[:, cols]) for key in split(source_refs, lengths, cols, False)] for cols in columns]
+            rounded, totals, kept = [], [], []
+            for head in range(heads):
+                top = before = top_ref[head]
+                if true_maximum:
+                    for part, bias in zip(scores[head], biases):
+                        top = jnp.maximum(top, jnp.max(part, axis=0, keepdims=True) + bias)
+                weights = [jnp.exp2(part - (top - bias)) for part, bias in zip(scores[head], biases)]
+                kept.append(jnp.exp2(before - top) if true_maximum else 1.0)
+                totals.append(total_ref[head] * kept[head] + sum(jnp.sum(part, axis=0, keepdims=True) for part in weights))
+                rounded.append(jnp.concatenate([part.astype(query_ref.dtype) for part in weights]))
+            parts = [
+                weigh(jnp.concatenate(split(source_refs, lengths, cols, True)), rounded[head])
+                for head, cols in enumerate(columns)
+            ]
+            copies = []
+            for head, cols in enumerate(columns):
+                part = part_ref[head] * kept[head] + parts[head]
+                out_ref[head] = (part * (1.0 / totals[head])).astype(out_ref.dtype).T
                 copies.append(pltpu.make_async_copy(out_ref.at[head], out_hbm.at[:, cols], sems.at[head]))
                 copies[-1].start()
-            else:
-                outs[0][head], outs[1][head], outs[2][head] = top, total, part
-        for copy in copies:
-            copy.wait()
+            small = functools.reduce(jnp.logical_and, [total < SAFE_TOTAL for total in totals])
+            far = jnp.max(jnp.where(small, 0, 1))
+            for copy in copies:
+                copy.wait()
+            return far
+
+        far = run(False)
+
+        @pl.when(far > 0)
+        def _():
+            run(True)
 
     operands = [pltpu.with_memory_space_constraint(array, pltpu.VMEM) for array in (queries, *sources, *state)]
     return pl.pallas_call(
         kernel,
-        name="finish" if last else "join",
-        compiler_params=ROOM,
-        out_shape=pltpu.HBM((rows, width), queries.dtype) if last else state_shapes(heads, rows),
+        name="finish",
+        compiler_params=ROOM,
+        out_shape=pltpu.HBM((rows, width), queries.dtype),
         in_specs=[IN_VMEM] * len(operands),
-        out_specs=ANYWHERE if last else [IN_VMEM] * 3,
-        scratch_shapes=[pltpu.VMEM((heads, rows, HD), queries.dtype), pltpu.SemaphoreType.DMA((heads,))] if last else [],
+        out_specs=ANYWHERE,
+        scratch_shapes=[pltpu.VMEM((heads, rows, HD), queries.dtype), pltpu.SemaphoreType.DMA((heads,))],
         cost_estimate=cost(rows, sum(lengths), width),
     )(*operands)
 
@@ -227,8 +268,8 @@
     incoming = [swap(rows, choice) for rows, choice in zip(outgoing, plan)]
     cut = max(0, len(plan) - 2)
     for number in range(cut):
-        state = join(queries, incoming[number : number + 1], plan[number : number + 1], state, False)
-    return join(queries, incoming[cut:], plan[cut:], state, True)[None, None]
+        state = join(queries, incoming[number], plan[number], state)
+    return finish(queries, incoming[cut:], plan[cut:], state)[None, None]
 
 
 def solution(mesh):

time: 15.3 us -> 15.2 us (level)
  no operation moved by 1% of the time
where the time goes in v4:
time: 15.2 us; the launch traced here: 15.1 us
  waiting for transfers between devices  6.29 us (41%)
  starting transfers between devices  4.76 us (31%)
  Pallas kernels  3.98 us (26%)
    ppermute x3, waiting for transfers between devices, swap(): return lax.ppermute(value, AXES, pairs)  6.29 us
    ppermute x3, starting transfers between devices, swap(): return lax.ppermute(value, AXES, pairs)  4.76 us
    pallas_call x1, Pallas kernels, finish(): pl.pallas_call(kernel, name='finish', compiler_params=ROOM, out_shape=plt...  1.38 us
    pallas_call x1, Pallas kernels, pick(): pl.pallas_call(kernel, name='pick', compiler_params=ROOM, out_shape=[pltp...  1.24 us
    pallas_call x1, Pallas kernels, own(): pl.pallas_call(kernel, name='own', compiler_params=ROOM, out_shape=state_...  0.79 us
    pallas_call x1, Pallas kernels, join(): pl.pallas_call(kernel, name='join', compiler_params=ROOM, out_shape=state...  0.57 us
  transfers between devices with their start and end apart: 3, of which 2 were waited for; matrix products, arithmetic and copies ran while one was open for 0% of the time, Pallas kernels for 9%

profile of v4, /device:TPU:1, one launch (start us, length us, event | category | flops | bytes accessed | tf_op | source)
XLA Modules:
  0.0 15.1 jit_solution(5555442302903417915)
XLA Ops:
  0.0 0.0 copy-start
  0.0 1.2 %pick.1 = (bf16[256,768]{1,0:T(8,128)(2,1)S(1)}, bf16[256,768]{1,0:T(8,128)(2,1)S(1)}, bf16[256,768]{1,0:T(8,128)(2,1)S(1)}, bf16[256,768]{1,0:T(8,128)(2,1)S(1)}, bf16[256,768]{1,0:T(8,128)(2,1)S(1)}) custom-call(s32[2,2]{1,0:T(2,128)} %bitcast.11, s32[1,2]{1,0:T(1,128)} %bitcast.12, bf16[256,768]{1,0:T(8,128)(2,1)} %bitcast.9, bf16[256,768]{1,0:T(8,128)(2,1)} %bitcast.10), custom_call_target="tpu_custom_call" | custom-call | tf_op jit(solution)/shard_map/pick/pallas_call | solution.py:108
  1.2 2.1 %collective-permute-start.2 = (bf16[256,768]{1,0:T(8,128)(2,1)S(1)}, bf16[256,768]{1,0:T(8,128)(2,1)S(1)}, u32[]{:S(2)}, u32[]{:S(2)}) collective-permute-start(bf16[256,768]{1,0:T(8,128)(2,1)S(1)} %get-tuple-element.28), channel_id=1, source_target_pairs={{0,4},{1,3},{2,6},{3,1},{4,0},{5,7},{6,2},{7,5},{8,12},{9,11},{10,... | collective-permute-start | bytes 1179656 | tf_op jit(solution)/shard_map/ppermute | solution.py:55
  3.4 1.0 %collective-permute-start = (bf16[256,768]{1,0:T(8,128)(2,1)S(1)}, bf16[256,768]{1,0:T(8,128)(2,1)S(1)}, u32[]{:S(2)}, u32[]{:S(2)}) collective-permute-start(bf16[256,768]{1,0:T(8,128)(2,1)S(1)} %get-tuple-element.20), channel_id=1, source_target_pairs={{0,1},{1,0},{2,3},{3,2},{4,8},{5,9},{6,10},{7,11},{8,4},{9,5},{10,... | collective-permute-start | bytes 1179656 | tf_op jit(solution)/shard_map/ppermute | solution.py:55
  4.4 0.0 copy-done
  4.4 0.8 %own.1 = (f32[6,1,256]{2,1,0:T(1,128)S(1)}, f32[6,1,256]{2,1,0:T(1,128)S(1)}, f32[6,128,256]{2,1,0:T(8,128)S(1)}) custom-call(bf16[256,768]{1,0:T(8,128)(2,1)S(1)} %bitcast.6, bf16[256,768]{1,0:T(8,128)(2,1)S(1)} %get-tuple-element.22.key_ref, bf16[256,768]{1,0:T(8,128)(2,1)S(1)} %get-tuple-element.23.value_ref), custom_call_target="tpu_custom_call" | custom-call | tf_op jit(solution)/shard_map/own/pallas_call | solution.py:155
  5.2 1.6 %collective-permute-start.1 = (bf16[256,768]{1,0:T(8,128)(2,1)S(1)}, bf16[256,768]{1,0:T(8,128)(2,1)S(1)}, u32[]{:S(2)}, u32[]{:S(2)}) collective-permute-start(bf16[256,768]{1,0:T(8,128)(2,1)S(1)} %get-tuple-element.27), channel_id=1, source_target_pairs={{0,2},{1,5},{2,0},{3,7},{4,6},{5,1},{6,4},{7,3},{8,10},{9,13},{10,... | collective-permute-start | bytes 1179656 | tf_op jit(solution)/shard_map/ppermute | solution.py:55
  6.8 2.3 %collective-permute-done.2.source_ref = bf16[256,768]{1,0:T(8,128)(2,1)S(1)} collective-permute-done((bf16[256,768]{1,0:T(8,128)(2,1)S(1)}, bf16[256,768]{1,0:T(8,128)(2,1)S(1)}, u32[]{:S(2)}, u32[]{:S(2)}) %collective-permute-start.2) | collective-permute-done | bytes 393248 | tf_op jit(solution)/shard_map/ppermute | solution.py:55
  9.1 0.6 %join.1 = (f32[6,1,256]{2,1,0:T(1,128)S(1)}, f32[6,1,256]{2,1,0:T(1,128)S(1)}, f32[6,128,256]{2,1,0:T(8,128)S(1)}) custom-call(bf16[256,768]{1,0:T(8,128)(2,1)S(1)} %bitcast.7, bf16[256,768]{1,0:T(8,128)(2,1)S(1)} %collective-permute-done.2.source_ref, f32[6,1,256]{2,1,0:T(1,128)S(1)} %get-tuple-element.29.top_ref, ...), custom_call_target="tpu_custom_call" | custom-call | flops 100663296 | bytes 786432 | tf_op jit(solution)/shard_map/join/pallas_call | solution.py:191
  9.7 0.0 collective-permute-done.rest_0_
  9.7 4.0 %collective-permute-done.1.rest_1_ = bf16[256,768]{1,0:T(8,128)(2,1)S(1)} collective-permute-done((bf16[256,768]{1,0:T(8,128)(2,1)S(1)}, bf16[256,768]{1,0:T(8,128)(2,1)S(1)}, u32[]{:S(2)}, u32[]{:S(2)}) %collective-permute-start.1) | collective-permute-done | bytes 393248 | tf_op jit(solution)/shard_map/ppermute | solution.py:55
  13.7 1.4 %finish.1 = bf16[256,768]{1,0:T(8,128)(2,1)} custom-call(bf16[256,768]{1,0:T(8,128)(2,1)S(1)} %bitcast.8, bf16[256,768]{1,0:T(8,128)(2,1)S(1)} %collective-permute-done.rest_0_, bf16[256,768]{1,0:T(8,128)(2,1)S(1)} %collective-permute-done.1.rest_1_, f32[6,1,256]{2,1,0:T(1,128)S(1)} %get-tuple-element.32.rest_2_, ...), custom_call_target="tpu_custom_call" | custom-call | flops 201326592 | bytes 1179648 | tf_op jit(solution)/shard_map/finish/pallas_call | solution.py:248
Async XLA Ops:
  0.0 4.4 %copy-start = (bf16[1,1,256,768]{3,2,1,0:T(8,128)(2,1)S(1)}, bf16[1,1,256,768]{3,2,1,0:T(8,128)(2,1)}, u32[]{:S(2)}) copy-start(bf16[1,1,256,768]{3,2,1,0:T(8,128)(2,1)} %param.5) | copy-start | bytes 1179652
  1.2 7.9 %collective-permute-start.2 = (bf16[256,768]{1,0:T(8,128)(2,1)S(1)}, bf16[256,768]{1,0:T(8,128)(2,1)S(1)}, u32[]{:S(2)}, u32[]{:S(2)}) collective-permute-start(bf16[256,768]{1,0:T(8,128)(2,1)S(1)} %get-tuple-element.28), channel_id=1, source_target_pairs={{0,4},{1,3},{2,6},{3,1},{4,0},{5,7},{6,2},{7,5},{8,12},{9,11},{10,... | collective-permute-start | bytes 1179656 | tf_op jit(solution)/shard_map/ppermute | solution.py:55
  3.4 6.4 %collective-permute-start = (bf16[256,768]{1,0:T(8,128)(2,1)S(1)}, bf16[256,768]{1,0:T(8,128)(2,1)S(1)}, u32[]{:S(2)}, u32[]{:S(2)}) collective-permute-start(bf16[256,768]{1,0:T(8,128)(2,1)S(1)} %get-tuple-element.20), channel_id=1, source_target_pairs={{0,1},{1,0},{2,3},{3,2},{4,8},{5,9},{6,10},{7,11},{8,4},{9,5},{10,... | collective-permute-start | bytes 1179656 | tf_op jit(solution)/shard_map/ppermute | solution.py:55
  5.2 8.5 %collective-permute-start.1 = (bf16[256,768]{1,0:T(8,128)(2,1)S(1)}, bf16[256,768]{1,0:T(8,128)(2,1)S(1)}, u32[]{:S(2)}, u32[]{:S(2)}) collective-permute-start(bf16[256,768]{1,0:T(8,128)(2,1)S(1)} %get-tuple-element.27), channel_id=1, source_target_pairs={{0,2},{1,5},{2,0},{3,7},{4,6},{5,1},{6,4},{7,3},{8,10},{9,13},{10,... | collective-permute-start | bytes 1179656 | tf_op jit(solution)/shard_map/ppermute | solution.py:55

commit v5 on v4

--- a/solution.py
+++ b/solution.py
@@ -13,6 +13,8 @@
 HD = 128
 MASKED = -1e30
 SAFE_TOTAL = 2.0**90
+LAST_SHARE = 3
+LAST_SOURCES = 3
 TO_EXP2 = math.log2(math.e) / math.sqrt(HD)
 AXES = ("tm", "band", "head")
 ROOM = pltpu.CompilerParams(vmem_limit_bytes=16 * 1024 * 1024)
@@ -71,13 +73,13 @@
     return jnp.where(goes_up(axis, phase), jnp.where(here < size - 1, 1, 0), jnp.where(here > 0, 1, 0))
 
 
-def pick(plan, adj_mask, border_blocks, keys, values):
-    width = keys.shape[1]
+def pick(plan, pieces, adj_mask, border_blocks, keys, values):
     blocks = adj_mask.shape[1]
     counts = [border_blocks.shape[0] if choice[0][0] == "band" else 1 for choice in plan]
+    shapes = [(2 * count * BLK, piece.stop - piece.start) for count, cuts in zip(counts, pieces) for piece in cuts]
 
     def kernel(adj_hbm, border_hbm, key_hbm, value_hbm, *rest):
-        outs, (key_ref, value_ref, adj_ref, border_ref, sems) = rest[: len(plan)], rest[len(plan) :]
+        outs, (key_ref, value_ref, adj_ref, border_ref, sems) = iter(rest[: len(shapes)]), rest[len(shapes) :]
         pairs = ((adj_hbm, adj_ref), (border_hbm, border_ref), (key_hbm, key_ref), (value_hbm, value_ref))
         copies = [pltpu.make_async_copy(*pair, sems.at[number]) for number, pair in enumerate(pairs)]
         for copy in copies:
@@ -85,7 +87,8 @@
         for copy in copies[:2]:
             copy.wait()
         chosen = []
-        for out, choice, count in zip(outs, plan, counts):
+        for choice, count, cuts in zip(plan, counts, pieces):
+            cut_outs = [(piece, next(outs)) for piece in cuts]
             for entry in range(count):
 
                 def block(axis, phase):
@@ -96,25 +99,27 @@
                     return sum(number * adj_ref[row, number] for number in range(1, blocks))
 
                 rows = pl.ds(pl.multiple_of(either(choice, block) * BLK, BLK), BLK)
-                chosen.append((out, rows, entry * BLK, (count + entry) * BLK))
+                chosen += [(out, piece, rows, entry * BLK, (count + entry) * BLK) for piece, out in cut_outs]
         copies[2].wait()
-        for out, rows, place, _ in chosen:
-            out[pl.ds(place, BLK)] = key_ref[rows]
+        for out, piece, rows, place, _ in chosen:
+            out[pl.ds(place, BLK)] = key_ref[rows, piece]
         copies[3].wait()
-        for out, rows, _, place in chosen:
-            out[pl.ds(place, BLK)] = value_ref[rows]
+        for out, piece, rows, _, place in chosen:
+            out[pl.ds(place, BLK)] = value_ref[rows, piece]
 
     arrays = (adj_mask, border_blocks, keys, values)
-    return pl.pallas_call(
+    *outgoing, keys, values = pl.pallas_call(
         kernel,
         name="pick",
         compiler_params=ROOM,
-        out_shape=[pltpu.VMEM((2 * count * BLK, width), keys.dtype) for count in counts]
+        out_shape=[pltpu.VMEM(shape, keys.dtype) for shape in shapes]
         + [pltpu.VMEM(array.shape, array.dtype) for array in arrays[2:]],
         in_specs=[ANYWHERE] * 4,
-        out_specs=[IN_VMEM] * (len(plan) + 2),
+        out_specs=[IN_VMEM] * (len(shapes) + 2),
         scratch_shapes=[pltpu.SMEM(array.shape, array.dtype) for array in arrays[:2]] + [pltpu.SemaphoreType.DMA((4,))],
     )(*(pltpu.with_memory_space_constraint(array, pltpu.HBM) for array in arrays))
+    outgoing = iter(outgoing)
+    return [[next(outgoing) for _ in cuts] for cuts in pieces], keys, values
 
 
 def score(key, query):
@@ -161,10 +166,6 @@
         out_specs=[IN_VMEM] * 3,
 
     )(*(pltpu.with_memory_space_constraint(array, pltpu.VMEM) for array in (queries, keys, values)))
-
-
-def split(refs, lengths, cols, values):
-    return [ref[length:, cols] if values else ref[:length, cols] for ref, length in zip(refs, lengths)]
 
 
 def join(queries, source, choice, state):
@@ -199,77 +200,99 @@
     )(*operands)
 
 
-def finish(queries, sources, choices, state):
+def finish(queries, sources, choices, state, first, earlier):
     rows, width = queries.shape
-    heads = width // HD
     count = len(sources)
     lengths = [source.shape[0] // 2 for source in sources]
+    heads = range(first, first + sources[-1].shape[1] // HD)
+    whole = earlier is not None
+
+    def columns(head):
+        return slice(head * HD, (head + 1) * HD)
 
     def kernel(query_ref, *rest):
-        source_refs, (top_ref, total_ref, part_ref, out_hbm, out_ref, sems) = rest[:count], rest[count:]
+        source_refs, (top_ref, total_ref, part_ref, *rest) = rest[:count], rest[count:]
+        if whole:
+            earlier_ref, out_hbm, out_ref, sems = rest
+            sent = [pltpu.make_async_copy(earlier_ref.at[head], out_hbm.at[:, columns(head)], sems.at[head]) for head in range(first)]
+            for copy in sent:
+                copy.start()
+        else:
+            (out_ref,), sent = rest, []
         biases = [jnp.where(either(choice, has_partner) == 1, 0.0, MASKED).astype(jnp.float32) for choice in choices]
-        columns = [slice(head * HD, (head + 1) * HD) for head in range(heads)]
-
-        def run(true_maximum):
-            scores = [[score(key, query_ref[:, cols]) for key in split(source_refs, lengths, cols, False)] for cols in columns]
-            rounded, totals, kept = [], [], []
-            for head in range(heads):
-                top = before = top_ref[head]
+
+        def held(head, values):
+            cut = [columns(head if ref.shape[1] == width else head - first) for ref in source_refs]
+            return [
+                ref[length:, cols] if values else ref[:length, cols] for ref, length, cols in zip(source_refs, lengths, cut)
+            ]
+
+        def run(true_maximum, sent):
+            scores = [[score(key, query_ref[:, columns(head)]) for key in held(head, False)] for head in heads]
+            rounded, totals, before = [], [], []
+            for head, parts in zip(heads, scores):
+                top, total, part = top_ref[head], total_ref[head], part_ref[head]
                 if true_maximum:
-                    for part, bias in zip(scores[head], biases):
-                        top = jnp.maximum(top, jnp.max(part, axis=0, keepdims=True) + bias)
-                weights = [jnp.exp2(part - (top - bias)) for part, bias in zip(scores[head], biases)]
-                kept.append(jnp.exp2(before - top) if true_maximum else 1.0)
-                totals.append(total_ref[head] * kept[head] + sum(jnp.sum(part, axis=0, keepdims=True) for part in weights))
-                rounded.append(jnp.concatenate([part.astype(query_ref.dtype) for part in weights]))
-            parts = [
-                weigh(jnp.concatenate(split(source_refs, lengths, cols, True)), rounded[head])
-                for head, cols in enumerate(columns)
-            ]
-            copies = []
-            for head, cols in enumerate(columns):
-                part = part_ref[head] * kept[head] + parts[head]
-                out_ref[head] = (part * (1.0 / totals[head])).astype(out_ref.dtype).T
-                copies.append(pltpu.make_async_copy(out_ref.at[head], out_hbm.at[:, cols], sems.at[head]))
-                copies[-1].start()
+                    for scored, bias in zip(parts, biases):
+                        top = jnp.maximum(top, jnp.max(scored, axis=0, keepdims=True) + bias)
+                    kept = jnp.exp2(top_ref[head] - top)
+                    total, part = total * kept, part * kept
+                weights = [jnp.exp2(scored - (top - bias)) for scored, bias in zip(parts, biases)]
+                totals.append(total + sum(jnp.sum(weight, axis=0, keepdims=True) for weight in weights))
+                before.append(part)
+                rounded.append(jnp.concatenate([weight.astype(query_ref.dtype) for weight in weights]))
+            new = [weigh(jnp.concatenate(held(head, True)), weights) for head, weights in zip(heads, rounded)]
+            copies = list(sent)
+            for place, head in enumerate(heads):
+                out_ref[place] = ((before[place] + new[place]) * (1.0 / totals[place])).astype(out_ref.dtype).T
+                if whole:
+                    copies.append(pltpu.make_async_copy(out_ref.at[place], out_hbm.at[:, columns(head)], sems.at[head]))
+                    copies[-1].start()
             small = functools.reduce(jnp.logical_and, [total < SAFE_TOTAL for total in totals])
             far = jnp.max(jnp.where(small, 0, 1))
             for copy in copies:
                 copy.wait()
             return far
 
-        far = run(False)
+        far = run(False, sent)
 
         @pl.when(far > 0)
         def _():
-            run(True)
-
-    operands = [pltpu.with_memory_space_constraint(array, pltpu.VMEM) for array in (queries, *sources, *state)]
+            run(True, [])
+
+    given = (queries, *sources, *state, *([earlier] if whole else []))
+    operands = [pltpu.with_memory_space_constraint(array, pltpu.VMEM) for array in given]
+    out_ref = pltpu.VMEM((len(heads), rows, HD), queries.dtype)
     return pl.pallas_call(
         kernel,
-        name="finish",
+        name="finish" if whole else "settle",
         compiler_params=ROOM,
-        out_shape=pltpu.HBM((rows, width), queries.dtype),
+        out_shape=pltpu.HBM((rows, width), queries.dtype) if whole else out_ref,
         in_specs=[IN_VMEM] * len(operands),
-        out_specs=ANYWHERE,
-        scratch_shapes=[pltpu.VMEM((heads, rows, HD), queries.dtype), pltpu.SemaphoreType.DMA((heads,))],
-        cost_estimate=cost(rows, sum(lengths), width),
+        out_specs=ANYWHERE if whole else IN_VMEM,
+        scratch_shapes=[out_ref, pltpu.SemaphoreType.DMA((heads.stop,))] if whole else [],
+        cost_estimate=cost(rows, sum(lengths), len(heads) * HD),
     )(*operands)
 
 
 def per_device(queries, keys, values, adj_mask, border_blocks):
     queries, keys, values = queries[0, 0], keys[0, 0], values[0, 0]
     border_blocks = border_blocks[0, 0].T
+    width = queries.shape[1]
+    early = width // HD - width // HD // LAST_SHARE
     plan = swap_plan({axis: lax.axis_size(axis) for axis in AXES}, border_blocks.shape[0])
-    *outgoing, keys, values = pick(plan, adj_mask[0, 0], border_blocks, keys, values)
+    cut = max(0, len(plan) - 2)
+    pieces = [(slice(0, width),)] * cut + [(slice(0, early * HD), slice(early * HD, width))] * (len(plan) - cut)
+    outgoing, keys, values = pick(plan, pieces, adj_mask[0, 0], border_blocks, keys, values)
     state = own(queries, keys, values)
     for number in range(2, len(plan)):
         outgoing[number], state = lax.optimization_barrier((outgoing[number], state))
-    incoming = [swap(rows, choice) for rows, choice in zip(outgoing, plan)]
-    cut = max(0, len(plan) - 2)
-    for number in range(cut):
-        state = join(queries, incoming[number], plan[number], state)
-    return finish(queries, incoming[cut:], plan[cut:], state)[None, None]
+    incoming = [[swap(rows, choice) for rows in parts] for parts, choice in zip(outgoing, plan)]
+    last = max(0, len(plan) - LAST_SOURCES)
+    for number in range(last):
+        state = join(queries, incoming[number][0], plan[number], state)
+    settled = finish(queries, [parts[0] for parts in incoming[last:]], plan[last:], state, 0, None)
+    return finish(queries, [parts[-1] for parts in incoming[last:]], plan[last:], state, early, settled)[None, None]
 
 
 def solution(mesh):

time: 15.2 us -> 15 us (0.987)
  waiting for transfers between devices: 6.29 us -> 4.88 us
  starting transfers between devices: 4.76 us -> 6.06 us
    ppermute x3 -> x5, waiting for transfers between devices: 6.29 us -> 4.88 us  [swap(): return lax.ppermute(value, AXES, pairs)]
    ppermute x3 -> x5, starting transfers between devices: 4.76 us -> 6.06 us  [swap(): return lax.ppermute(value, AXES, pairs)]
  transfers between devices with their start and end apart: 3 -> 5, of which waited for: 2 -> 2; matrix products, arithmetic and copies ran while one was open for 0% -> 0% of each run, Pallas kernels for 9% -> 10%
where the time goes in v5:
time: 15 us; the launch traced here: 14.9 us
  starting transfers between devices  6.06 us (40%)
  waiting for transfers between devices  4.88 us (33%)
  Pallas kernels  3.93 us (26%)
    ppermute x5, starting transfers between devices, swap(): return lax.ppermute(value, AXES, pairs)  6.06 us
    ppermute x5, waiting for transfers between devices, swap(): return lax.ppermute(value, AXES, pairs)  4.88 us
    pallas_call x2, Pallas kernels, finish(): pl.pallas_call(kernel, name='finish' if whole else 'settle', compiler_par...  1.9 us
    pallas_call x1, Pallas kernels, pick(): pl.pallas_call(kernel, name='pick', compiler_params=ROOM, out_shape=[pltp...  1.24 us
    pallas_call x1, Pallas kernels, own(): pl.pallas_call(kernel, name='own', compiler_params=ROOM, out_shape=state_...  0.79 us
  transfers between devices with their start and end apart: 5, of which 2 were waited for; matrix products, arithmetic and copies ran while one was open for 0% of the time, Pallas kernels for 10%

profile of v5, /device:TPU:1, one launch (start us, length us, event | category | flops | bytes accessed | tf_op | source)
XLA Modules:
  0.0 14.9 jit_solution(17433146885489995097)
XLA Ops:
  0.0 0.0 copy-start
  0.0 1.2 %pick.1 = (bf16[256,768]{1,0:T(8,128)(2,1)S(1)}, bf16[256,512]{1,0:T(8,128)(2,1)S(1)}, bf16[256,256]{1,0:T(8,128)(2,1)S(1)}, bf16[256,512]{1,0:T(8,128)(2,1)S(1)...) custom-call(s32[2,2]{1,0:T(2,128)} %bitcast.11, s32[1,2]{1,0:T(1,128)} %bitcast.12, ...), custom_call_target="tpu_custom_call" | custom-call | tf_op jit(solution)/shard_map/pick/pallas_call | solution.py:111
  1.2 2.1 %collective-permute-start = (bf16[256,768]{1,0:T(8,128)(2,1)S(1)}, bf16[256,768]{1,0:T(8,128)(2,1)S(1)}, u32[]{:S(2)}, u32[]{:S(2)}) collective-permute-start(bf16[256,768]{1,0:T(8,128)(2,1)S(1)} %get-tuple-element.20), channel_id=1, source_target_pairs={{0,4},{1,3},{2,6},{3,1},{4,0},{5,7},{6,2},{7,5},{8,12},{9,11},{10,... | collective-permute-start | bytes 1179656 | tf_op jit(solution)/shard_map/ppermute | solution.py:57
  3.4 1.0 %collective-permute-start.3 = (bf16[256,512]{1,0:T(8,128)(2,1)S(1)}, bf16[256,512]{1,0:T(8,128)(2,1)S(1)}, u32[]{:S(2)}, u32[]{:S(2)}) collective-permute-start(bf16[256,512]{1,0:T(8,128)(2,1)S(1)} %get-tuple-element.33), channel_id=1, source_target_pairs={{0,1},{1,0},{2,3},{3,2},{4,8},{5,9},{6,10},{7,11},{8,4},{9,5},{10,... | collective-permute-start | bytes 786440 | tf_op jit(solution)/shard_map/ppermute | solution.py:57
  4.4 0.0 copy-done
  4.4 0.8 %own.1 = (f32[6,1,256]{2,1,0:T(1,128)S(1)}, f32[6,1,256]{2,1,0:T(1,128)S(1)}, f32[6,128,256]{2,1,0:T(8,128)S(1)}) custom-call(bf16[256,768]{1,0:T(8,128)(2,1)S(1)} %bitcast.6, bf16[256,768]{1,0:T(8,128)(2,1)S(1)} %get-tuple-element.24.key_ref, bf16[256,768]{1,0:T(8,128)(2,1)S(1)} %get-tuple-element.25.value_ref), custom_call_target="tpu_custom_call" | custom-call | tf_op jit(solution)/shard_map/own/pallas_call | solution.py:160
  5.2 1.6 %collective-permute-start.4 = (bf16[256,512]{1,0:T(8,128)(2,1)S(1)}, bf16[256,512]{1,0:T(8,128)(2,1)S(1)}, u32[]{:S(2)}, u32[]{:S(2)}) collective-permute-start(bf16[256,512]{1,0:T(8,128)(2,1)S(1)} %get-tuple-element.34), channel_id=1, source_target_pairs={{0,2},{1,5},{2,0},{3,7},{4,6},{5,1},{6,4},{7,3},{8,10},{9,13},{10,... | collective-permute-start | bytes 786440 | tf_op jit(solution)/shard_map/ppermute | solution.py:57
  6.8 0.0 collective-permute-start.1
  6.8 1.3 %collective-permute-start.2 = (bf16[256,256]{1,0:T(8,128)(2,1)S(1)}, bf16[256,256]{1,0:T(8,128)(2,1)S(1)}, u32[]{:S(2)}, u32[]{:S(2)}) collective-permute-start(bf16[256,256]{1,0:T(8,128)(2,1)S(1)} %get-tuple-element.29), channel_id=1, source_target_pairs={{0,2},{1,5},{2,0},{3,7},{4,6},{5,1},{6,4},{7,3},{8,10},{9,13},{10,... | collective-permute-start | bytes 393224 | tf_op jit(solution)/shard_map/ppermute | solution.py:57
  8.1 0.0 collective-permute-done.3.rest_1_
  8.1 4.5 %collective-permute-done.4.rest_2_ = bf16[256,512]{1,0:T(8,128)(2,1)S(1)} collective-permute-done((bf16[256,512]{1,0:T(8,128)(2,1)S(1)}, bf16[256,512]{1,0:T(8,128)(2,1)S(1)}, u32[]{:S(2)}, u32[]{:S(2)}) %collective-permute-start.4) | collective-permute-done | bytes 262176 | tf_op jit(solution)/shard_map/ppermute | solution.py:57
  12.6 0.0 collective-permute-done.rest_0_
  12.6 0.7 %settle.1.rest_6_ = bf16[4,256,128]{2,1,0:T(8,128)(2,1)S(1)} custom-call(bf16[256,768]{1,0:T(8,128)(2,1)S(1)} %bitcast.7, bf16[256,768]{1,0:T(8,128)(2,1)S(1)} %collective-permute-done.rest_0_, bf16[256,512]{1,0:T(8,128)(2,1)S(1)} %collective-permute-done.3.rest_1_, bf16[256,512]{1,0:T(8,128)(2,1)S(1)} %collective-permute-done.4.rest_2_, ...), custom_call_target="tpu_custom_call" | custom-call | flops 201326592 | bytes 1048576 | tf_op jit(solution)/shard_map/settle/pallas_call | solution.py:266
  13.2 0.0 collective-permute-done.1.rest_1_
  13.3 0.4 %collective-permute-done.2.rest_2_ = bf16[256,256]{1,0:T(8,128)(2,1)S(1)} collective-permute-done((bf16[256,256]{1,0:T(8,128)(2,1)S(1)}, bf16[256,256]{1,0:T(8,128)(2,1)S(1)}, u32[]{:S(2)}, u32[]{:S(2)}) %collective-permute-start.2) | collective-permute-done | bytes 131104 | tf_op jit(solution)/shard_map/ppermute | solution.py:57
  13.7 1.2 %finish.1 = bf16[256,768]{1,0:T(8,128)(2,1)} custom-call(bf16[256,768]{1,0:T(8,128)(2,1)S(1)} %bitcast.8, bf16[256,768]{1,0:T(8,128)(2,1)S(1)} %collective-permute-done.rest_0_, bf16[256,256]{1,0:T(8,128)(2,1)S(1)} %collective-permute-done.1.rest_1_, bf16[256,256]{1,0:T(8,128)(2,1)S(1)} %collective-permute-done.2.rest_2_, ...), custom_call_target="tpu_custom_call" | custom-call | flops 100663296 | bytes 524288 | tf_op jit(solution)/shard_map/finish/pallas_call | solution.py:266
Async XLA Ops:
  0.0 4.4 %copy-start = (bf16[1,1,256,768]{3,2,1,0:T(8,128)(2,1)S(1)}, bf16[1,1,256,768]{3,2,1,0:T(8,128)(2,1)}, u32[]{:S(2)}) copy-start(bf16[1,1,256,768]{3,2,1,0:T(8,128)(2,1)} %param.5) | copy-start | bytes 1179652
  1.2 11.3 %collective-permute-start = (bf16[256,768]{1,0:T(8,128)(2,1)S(1)}, bf16[256,768]{1,0:T(8,128)(2,1)S(1)}, u32[]{:S(2)}, u32[]{:S(2)}) collective-permute-start(bf16[256,768]{1,0:T(8,128)(2,1)S(1)} %get-tuple-element.20), channel_id=1, source_target_pairs={{0,4},{1,3},{2,6},{3,1},{4,0},{5,7},{6,2},{7,5},{8,12},{9,11},{10,... | collective-permute-start | bytes 1179656 | tf_op jit(solution)/shard_map/ppermute | solution.py:57
  3.4 4.8 %collective-permute-start.3 = (bf16[256,512]{1,0:T(8,128)(2,1)S(1)}, bf16[256,512]{1,0:T(8,128)(2,1)S(1)}, u32[]{:S(2)}, u32[]{:S(2)}) collective-permute-start(bf16[256,512]{1,0:T(8,128)(2,1)S(1)} %get-tuple-element.33), channel_id=1, source_target_pairs={{0,1},{1,0},{2,3},{3,2},{4,8},{5,9},{6,10},{7,11},{8,4},{9,5},{10,... | collective-permute-start | bytes 786440 | tf_op jit(solution)/shard_map/ppermute | solution.py:57
  5.2 7.4 %collective-permute-start.4 = (bf16[256,512]{1,0:T(8,128)(2,1)S(1)}, bf16[256,512]{1,0:T(8,128)(2,1)S(1)}, u32[]{:S(2)}, u32[]{:S(2)}) collective-permute-start(bf16[256,512]{1,0:T(8,128)(2,1)S(1)} %get-tuple-element.34), channel_id=1, source_target_pairs={{0,2},{1,5},{2,0},{3,7},{4,6},{5,1},{6,4},{7,3},{8,10},{9,13},{10,... | collective-permute-start | bytes 786440 | tf_op jit(solution)/shard_map/ppermute | solution.py:57
  6.8 6.4 %collective-permute-start.1 = (bf16[256,256]{1,0:T(8,128)(2,1)S(1)}, bf16[256,256]{1,0:T(8,128)(2,1)S(1)}, u32[]{:S(2)}, u32[]{:S(2)}) collective-permute-start(bf16[256,256]{1,0:T(8,128)(2,1)S(1)} %get-tuple-element.21), channel_id=1, source_target_pairs={{0,1},{1,0},{2,3},{3,2},{4,8},{5,9},{6,10},{7,11},{8,4},{9,5},{10,... | collective-permute-start | bytes 393224 | tf_op jit(solution)/shard_map/ppermute | solution.py:57
  6.8 6.9 %collective-permute-start.2 = (bf16[256,256]{1,0:T(8,128)(2,1)S(1)}, bf16[256,256]{1,0:T(8,128)(2,1)S(1)}, u32[]{:S(2)}, u32[]{:S(2)}) collective-permute-start(bf16[256,256]{1,0:T(8,128)(2,1)S(1)} %get-tuple-element.29), channel_id=1, source_target_pairs={{0,2},{1,5},{2,0},{3,7},{4,6},{5,1},{6,4},{7,3},{8,10},{9,13},{10,... | collective-permute-start | bytes 393224 | tf_op jit(solution)/shard_map/ppermute | solution.py:57
